TPU v7x, 512 devices: a whole 4x8x8 slice. The times are simulated.
512 devices in a mesh: row: 16 (over z, core), col: 32 (over y, x).
Axes of the slice: x: 4, y: 8, z: 8, core: 2. Of those that a mesh axis runs over, the one named last changes fastest.
Arguments:
- query_tokens: bfloat16 [512, 32, 128], P('row'), may hold values from -14 to 14
- query_lengths: int32 [512], P('row'), may hold values from 8 to 32
- passage_tokens: bfloat16 [4096, 176, 128], P(('col', 'row')), may hold values from -8 to 8
- passage_lengths: int32 [4096], P(('col', 'row')), may hold values from 44 to 176
- student_queries: bfloat16 [512, 768], P('row', 'col'), may hold values from -28 to 28
- student_passages: bfloat16 [4096, 768], P('col', 'row'), may hold values from -0.21875 to 0.21875
- positives: int32 [512], P('row'), may hold values from 0 to 4095
Outputs:
- query_grads: float32 [512, 768], P('row', 'col')
- passage_grads: float32 [4096, 768], P('col', 'row')
- loss: float32 [], replicated
All inputs are finite; a program needn't handle non-finite values.
Results may differ from a plain program's by a relative error of at most 0.00045.
Values may be sent and summed in bfloat16 or wider, within the bound.
A program may use at most 64 MiB of HBM per device.

v0:
```python
import jax
import jax.numpy as jnp
from jax import lax
from jax.sharding import PartitionSpec as P

NEG = -1e30
SCALE = 4.0


def token_block_max(query_rows, tokens, lengths):
    count = tokens.shape[1]
    result = jnp.full((query_rows.shape[0], tokens.shape[0]), NEG, jnp.float32)
    for first in range(0, count, 16):
        span = min(16, count - first)
        block = tokens[:, first : first + span, :]
        sims = jnp.einsum("ie,pte->itp", query_rows, block, preferred_element_type=jnp.float32)
        valid = (first + jnp.arange(span))[:, None] < lengths[None, :]
        sims = jnp.where(valid[None], sims, NEG)
        result = jnp.maximum(result, jnp.max(sims, axis=1))
    return result


def shards(
    query_tokens,
    query_lengths,
    passage_tokens,
    passage_lengths,
    student_queries,
    student_passages,
    positives,
):
    query_block = query_tokens.shape[0]
    slots = query_tokens.shape[1]
    width = query_tokens.shape[2]
    local_passages = passage_tokens.shape[0]
    row_count = lax.axis_size("row")
    passage_block = local_passages * row_count
    total_queries = query_block * row_count
    full_queries = lax.all_gather(student_queries, "col", axis=1, tiled=True)
    full_passages = lax.all_gather(student_passages, "row", axis=1, tiled=True)
    query_rows = query_tokens.reshape(query_block * slots, width)
    found = token_block_max(
        query_rows,
        lax.all_gather(passage_tokens, "row", axis=0, tiled=True),
        lax.all_gather(passage_lengths, "row", axis=0, tiled=True),
    )
    maxima = found
    maxima = maxima.reshape(query_block, slots, passage_block)
    query_mask = (jnp.arange(slots)[None, :] < query_lengths[:, None]).astype(jnp.float32)
    teacher = jnp.sum(maxima * query_mask[:, :, None], axis=1)
    student = SCALE * jnp.dot(full_queries, full_passages.T, preferred_element_type=jnp.float32)
    passage_start = lax.axis_index("col") * passage_block
    onehot = (passage_start + jnp.arange(passage_block))[None, :] == positives[:, None]
    positive_part = jnp.sum(jnp.where(onehot, student, 0.0), axis=1)
    local_teacher_max = jnp.max(teacher, axis=1)
    local_student_max = jnp.max(student, axis=1)
    teacher_max, student_max = lax.pmax((local_teacher_max, local_student_max), "col")
    teacher_exp = jnp.exp(teacher - teacher_max[:, None])
    student_exp = jnp.exp(student - student_max[:, None])
    teacher_sum, student_sum, cross, positive_score = lax.psum(
        (
            jnp.sum(teacher_exp, axis=1),
            jnp.sum(student_exp, axis=1),
            jnp.sum(teacher_exp * (teacher - student), axis=1),
            positive_part,
        ),
        "col",
    )
    teacher_lse = teacher_max + jnp.log(teacher_sum)
    student_lse = student_max + jnp.log(student_sum)
    per_query = cross / teacher_sum - teacher_lse + 2.0 * student_lse - positive_score
    loss = lax.psum(jnp.sum(per_query) / total_queries, "row")
    teacher_probs = teacher_exp / teacher_sum[:, None]
    student_probs = student_exp / student_sum[:, None]
    slope = (2.0 * student_probs - teacher_probs - onehot.astype(jnp.float32)) / total_queries
    query_terms = SCALE * jnp.dot(
        slope, full_passages.astype(jnp.float32), precision=lax.Precision.HIGHEST
    )
    passage_terms = SCALE * jnp.dot(
        slope.T, full_queries.astype(jnp.float32), precision=lax.Precision.HIGHEST
    )
    query_grads = lax.psum_scatter(query_terms, "col", scatter_dimension=1, tiled=True)
    passage_grads = lax.psum_scatter(passage_terms, "row", scatter_dimension=1, tiled=True)
    return (query_grads, passage_grads, loss)


def solution(mesh):
    return jax.shard_map(
        shards,
        mesh=mesh,
        in_specs=(
            P("row", None, None),
            P("row"),
            P(("col", "row"), None, None),
            P(("col", "row")),
            P("row", "col"),
            P("col", "row"),
            P("row"),
        ),
        out_specs=(P("row", "col"), P("col", "row"), P()),
        check_vma=False,
    )
```

profile of v0, /device:TPU:1, one launch (start us, length us, event | category | flops | bytes accessed | tf_op | source)
XLA Modules:
  0.0 526.1 jit_solution(7206235024162393298)
XLA Ops:
  7.2 1.8 copy.12
  9.1 1.3 dynamic-slice
  11.1 0.9 dynamic-update-slice
  11.9 17.9 %all-reduce = s32[128]{0:T(128)S(1)} all-reduce(s32[128]{0:T(128)S(1)} %dynamic-update-slice), channel_id=1, replica_groups=mesh['row'=16,'col'=32] {'row'}, use_global_device_ids=true, to_apply=%add | all-reduce | flops 128 | bytes 1024
  29.8 41.1 %all_gather.12 = bf16[32,768]{0,1:T(8,128)(2,1)S(1)} all-gather(bf16[32,24]{0,1:T(8,128)(2,1)} %param.11), channel_id=1, replica_groups=mesh['row'=16,'col'=32] {'col'}, dimensions={1}, use_global_device_ids=true | all-gather | bytes 50688 | tf_op jit(solution)/shard_map/all_gather | solution.py:39
  71.0 25.7 %all_gather.13 = bf16[128,768]{0,1:T(8,128)(2,1)S(1)} all-gather(bf16[128,48]{0,1:T(8,128)(2,1)} %param.12), channel_id=1, replica_groups=mesh['row'=16,'col'=32] {'row'}, dimensions={1}, use_global_device_ids=true | all-gather | bytes 208896 | tf_op jit(solution)/shard_map/all_gather | solution.py:40
  97.9 2.5 fusion
  100.7 1.5 fusion.1
  102.2 1.5 fusion.10
  103.7 1.5 fusion.2
  105.3 1.5 fusion.3
  106.8 1.5 fusion.4
  108.3 1.5 fusion.5
  109.8 1.5 fusion.6
  111.3 1.5 fusion.7
  112.9 1.5 fusion.8
  114.4 1.5 fusion.9
  117.0 57.1 %all-reduce.3 = (f32[32]{0:T(128)S(1)}, f32[32]{0:T(128)S(1)}) all-reduce(f32[32]{0:T(128)S(1)} %reduce_max.150, f32[32]{0:T(128)S(1)} %get-tuple-element.24), channel_id=1, replica_groups=mesh['row'=16,'col'=32] {'col'}, use_global_device_ids=true, to_apply=%region_17.18 | all-reduce | flops 64 | bytes 512 | tf_op jit(solution)/shard_map/pmax | solution.py:57
  174.4 56.2 %all-reduce.2 = (f32[32]{0:T(128)S(1)}, f32[32]{0:T(128)S(1)}, f32[32]{0:T(128)S(1)}, f32[32]{0:T(128)S(1)}) all-reduce(f32[32]{0:T(128)S(1)} %get-tuple-element.4, f32[32]{0:T(128)S(1)} %get-tuple-element.6, f32[32]{0:T(128)S(1)} %get-tuple-element.5, f32[32]{0:T(128)S(1)} %get-tuple-element.3), channel_id=1, replica_groups=mesh['row'=16,'col'=32] {'col'}, use_global_device_ids=true, to_apply=%region_19.20 | all-reduce | flops 128 | bytes 1024 | tf_op jit(solution)/shard_map/psum | solution.py:60
  230.6 1.1 convolution_multiply_fusion.1
  231.8 1.1 convolution_multiply_fusion
  234.3 51.5 %psum.39 = f32[]{:T(128)} all-reduce(f32[]{:T(128)S(6)} %div.35), channel_id=1, replica_groups=mesh['row'=16,'col'=32] {'row'}, use_global_device_ids=true, to_apply=%region_27.28 | all-reduce | flops 1 | bytes 8 | tf_op jit(solution)/shard_map/psum | solution.py:72
  285.7 169.1 %reduce-scatter.7.cloned.1.call-done = f32[32,24]{0,1:T(8,128)} async-done(((f32[32,768]{0,1:T(8,128)}), f32[32,24]{0,1:T(8,128)}) %reduce-scatter.7.cloned.1.call-update) | async-done | bytes 3088
  454.9 64.7 %reduce-scatter.5.cloned.1.call-done = f32[128,48]{0,1:T(8,128)} async-done(((f32[128,768]{0,1:T(8,128)}), f32[128,48]{0,1:T(8,128)}) %reduce-scatter.5.cloned.1.call-update) | async-done | bytes 24592 | tf_op jit(solution)/shard_map/reduce_scatter | solution.py:83
  (29 shorter events, 3.6 us)
Async XLA Ops:
  7.2 90.8 %copy-start = (bf16[32,32,128]{2,1,0:T(8,128)(2,1)S(1)}, bf16[32,32,128]{2,1,0:T(8,128)(2,1)}, u32[]{:S(2)}) copy-start(bf16[32,32,128]{2,1,0:T(8,128)(2,1)} %param.7) | copy-start | bytes 786436
  7.2 90.7 %all-gather.2.cloned.1.call-start = ((), (), s32[]{:S(2)}) async-start(), calls=%async_computation.2 | async-start | bytes 6127616 | tf_op jit(solution)/shard_map/all_gather | solution.py:44
  9.1 445.8 %reduce-scatter.7.cloned.1.call-start = ((), (), s32[]{:S(2)}) async-start(), calls=%async_computation.4 | async-start | bytes 405504
  97.9 2.8 copy-start.2
  114.4 59.8 %copy-start.1 = (s32[32]{0:T(128)S(1)}, s32[32]{0:T(128)}, u32[]{:S(2)}) copy-start(s32[32]{0:T(128)} %param.13) | copy-start | bytes 388
  231.8 287.8 %reduce-scatter.5.cloned.1.call-start = ((), (), s32[]{:S(2)}) async-start(), calls=%async_computation.3 | async-start | bytes 417792 | tf_op jit(solution)/shard_map/reduce_scatter | solution.py:83
Sparse Core Ops, SparseCore 0:
  10.1 64.6 all-gather.1
  231.9 222.9 reduce-scatter.6
  458.2 61.2 reduce-scatter.4
where the time goes:
time: 528 us; the launch traced here: 526 us
  blocking collectives  250 us (47%)
  waiting for transfers between devices  234 us (44%)
  matrix products  20.2 us (4%)
  between operations  15.2 us (3%)
    unnamed x4, waiting for transfers between devices  169 us
    reduce_scatter x1, waiting for transfers between devices, shards(): lax.psum_scatter(passage_terms, 'row', scatter_dimension=1, tiled=True)  64.7 us
    pmax x1, blocking collectives, shards(): lax.pmax((local_teacher_max, local_student_max), 'col')  57.1 us
    psum x1, blocking collectives, shards(): lax.psum((jnp.sum(teacher_exp, axis=1), jnp.sum(student_exp, axis=1), jnp...  56.2 us
    psum x1, blocking collectives, shards(): loss = lax.psum(jnp.sum(per_query) / total_queries, 'row')  51.5 us
    all_gather x1, blocking collectives, shards(): full_queries = lax.all_gather(student_queries, 'col', axis=1, tiled=True)  41.1 us
    all_gather x1, blocking collectives, shards(): full_passages = lax.all_gather(student_passages, 'row', axis=1, tiled=True)  25.7 us
    unnamed x1, blocking collectives  17.9 us
  transfers between devices with their start and end apart: 3, of which 2 were waited for; matrix products, arithmetic and copies ran while one was open for 1% of the time, Pallas kernels for 0%

commit v1 on v0

v1 whole, which is shorter than its diff:
```python
import functools

import jax
import jax.numpy as jnp
from jax import lax
from jax.experimental import pallas as pl
from jax.experimental.pallas import tpu as pltpu
from jax.sharding import PartitionSpec as P

MESH = pl.DeviceIdType.MESH
SCALE = 4.0
X_CHIPS = 4
QB = 32
GROUPS = 128 // QB
BF = jnp.bfloat16
F32 = jnp.float32


def nt(a, b):
    return lax.dot_general(a, b, (((1,), (1,)), ((), ())), preferred_element_type=F32)


def nn(a, b):
    return lax.dot_general(a, b, (((1,), (0,)), ((), ())), preferred_element_type=F32)


def split2(v):
    hi = v.astype(BF)
    return hi, (v - hi.astype(F32)).astype(BF)


def spread(v):
    v = v + pltpu.roll(v, 64, 1)
    return v + pltpu.roll(v, 32, 1)


def kernel(
    R,
    C,
    qt_ref,
    qlen_ref,
    pt_ref,
    plen_ref,
    sq_ref,
    sp_ref,
    pos_ref,
    pg_ref,
    qg_ref,
    loss_ref,
    qraw,
    praw,
    qbuf,
    xbuf,
    sqx,
    spt,
    sst,
    sbuf,
    upz,
    vbuf,
    zag,
    zfull,
    sqr,
    tblk,
    town,
    tag,
    upt,
    ubuf,
    fin,
    in_sem,
    z_send,
    z_recv,
    xy_send,
    xy_recv,
    sib_send,
    sib_recv,
    many_send,
    many_recv,
):
    Z = R // 2
    XC = min(X_CHIPS, C)
    YC = C // XC
    L = qt_ref.shape[1]
    LP = pt_ref.shape[1]
    N = QB * L
    SL = N // 4
    HALF = SL // 2
    PB = 8 * R
    PR = C // R
    DR = 24 * PR
    T = R // GROUPS
    total = QB * R

    r = lax.axis_index("row")
    c = lax.axis_index("col")
    z = lax.div(r, 2)
    k = lax.rem(r, 2)
    x = lax.rem(c, XC)
    y = lax.div(c, XC)
    color = lax.rem(x + 2 * y, 4)

    def row_of(zz, kk):
        return lax.rem(zz + 2 * Z, Z) * 2 + kk

    def col_of(xx, yy):
        return lax.rem(yy + YC, YC) * XC + lax.rem(xx + XC, XC)

    def send(src, dst, s_sem, r_sem, **where):
        pltpu.make_async_remote_copy(
            src_ref=src, dst_ref=dst, send_sem=s_sem, recv_sem=r_sem, device_id=where, device_id_type=MESH
        ).start()

    def got(dst, r_sem):
        pltpu.make_async_remote_copy(
            src_ref=dst, dst_ref=dst, send_sem=r_sem, recv_sem=r_sem, device_id={"row": r}, device_id_type=MESH
        ).wait_recv()

    def left(src, s_sem):
        pltpu.make_async_remote_copy(
            src_ref=src, dst_ref=src, send_sem=s_sem, recv_sem=s_sem, device_id={"row": r}, device_id_type=MESH
        ).wait_send()

    q_in = pltpu.make_async_copy(qt_ref, qraw, in_sem.at[0])
    p_in = pltpu.make_async_copy(pt_ref, praw, in_sem.at[1])
    q_in.start()
    p_in.start()
    barrier = pltpu.get_barrier_semaphore()

    def greet_col(i, carry):
        pl.semaphore_signal(barrier, inc=1, device_id={"col": lax.rem(c + i, C)}, device_id_type=MESH)
        return carry

    def greet_row(i, carry):
        pl.semaphore_signal(barrier, inc=1, device_id={"row": lax.rem(r + i, R)}, device_id_type=MESH)
        return carry

    lax.fori_loop(1, C, greet_col, 0)
    lax.fori_loop(1, R, greet_row, 0)

    rows_p = lax.broadcasted_iota(jnp.int32, (PB, 128), 0)
    lane = lax.broadcasted_iota(jnp.int32, (1, 128), 1)
    lane_group = lax.div(lane, QB)

    def eye(n):
        a = lax.broadcasted_iota(jnp.int32, (n, n), 0)
        b = lax.broadcasted_iota(jnp.int32, (n, n), 1)
        return a, b

    a24, b24 = eye(24)
    sq_t = nt((a24 == b24).astype(BF), jnp.concatenate([sq_ref[...]] * GROUPS, axis=0))
    packed = jnp.zeros((8, 128), F32)
    for g in range(3):
        packed = jnp.where(lane_group == g, sq_t[8 * g : 8 * g + 8], packed)
    sqx[c] = packed
    aD, bD = eye(DR)
    source = lax.rem(lax.div(aD, 8), PR) * 24 + lax.div(aD, 8 * PR) * 8 + lax.rem(aD, 8)
    sp32 = sp_ref[...].astype(F32)
    sp_perm = jnp.concatenate(
        [sp32[8 * (2 * zz + kk) : 8 * (2 * zz + kk) + 8] for kk in range(2) for zz in range(Z)], axis=0
    ).astype(BF)
    spt[k, z] = nt((source == bD).astype(BF), sp_perm).astype(BF)

    q_in.wait()
    slot = lax.broadcasted_iota(jnp.int32, (L, 128), 0)
    q32 = jnp.stack(
        [jnp.where(slot < qlen_ref[i], qraw[i].astype(F32), 0.0) for i in range(QB)], axis=0
    )
    qbuf[r] = jnp.swapaxes(q32, 0, 1).reshape(N, 128).astype(BF)

    pl.semaphore_wait(barrier, C - 1 + R - 1)

    mine = pl.ds(pl.multiple_of(color * SL, SL), SL)
    mine_a = pl.ds(pl.multiple_of(color * SL, HALF), HALF)
    mine_b = pl.ds(pl.multiple_of(color * SL + HALF, HALF), HALF)

    def z_step(s):
        up = row_of(z - (s - 1), k)
        down = row_of(z + (s - 1), k)
        last = s == Z // 2
        a, b = (mine_a, mine_b) if last else (mine, mine)
        send(qbuf.at[up, a], qbuf.at[up, a], z_send.at[0, s - 1], z_recv.at[0, s - 1], row=row_of(z + 1, k))
        send(qbuf.at[down, b], qbuf.at[down, b], z_send.at[1, s - 1], z_recv.at[1, s - 1], row=row_of(z - 1, k))

    def z_got(s):
        last = s == Z // 2
        a, b = (mine_a, mine_b) if last else (mine, mine)
        got(qbuf.at[row_of(z - s, k), a], z_recv.at[0, s - 1])
        got(qbuf.at[row_of(z + s, k), b], z_recv.at[1, s - 1])

    offsets = []
    for s in range(1, Z // 2):
        offsets += [s, -s]
    offsets.append(Z // 2)

    def xy_regions():
        one = lax.rem(color + 3, 4) * SL
        two = lax.rem(color + 1, 4) * SL
        far = lax.rem(color + 2, 4) * SL
        return (
            pl.ds(pl.multiple_of(one, SL), SL),
            pl.ds(pl.multiple_of(two, SL), SL),
            pl.ds(pl.multiple_of(far, HALF), HALF),
            pl.ds(pl.multiple_of(far + HALF, HALF), HALF),
        )

    def xy_step(j):
        b = row_of(z + offsets[j], k)
        to = (col_of(x + 1, y), col_of(x - 1, y), col_of(x, y + 1), col_of(x, y - 1))
        for n, (part, peer) in enumerate(zip((mine, mine, mine_a, mine_b), to)):
            send(qbuf.at[b, part], qbuf.at[b, part], xy_send.at[n, j], xy_recv.at[n, j], col=peer)

    def xy_got(j):
        b = row_of(z + offsets[j], k)
        for n, part in enumerate(xy_regions()):
            got(qbuf.at[b, part], xy_recv.at[n, j])

    def sib_step(j):
        b = r if j == 0 else row_of(z + offsets[j - 1], k)
        send(qbuf.at[b], qbuf.at[b], sib_send.at[j], sib_recv.at[j], row=row_of(z, 1 - k))

    def sib_got(j):
        b = row_of(z, 1 - k) if j == 0 else row_of(z + offsets[j - 1], 1 - k)
        got(qbuf.at[b], sib_recv.at[j])
        return b

    def to_col(src_of, dst, n):
        def body(i, carry):
            peer = lax.rem(c + i, C)
            send(src_of(peer), dst, many_send.at[n], many_recv.at[n], col=peer)
            return carry

        lax.fori_loop(1, C, body, 0)

    def to_row(src_of, dst, n):
        def body(i, carry):
            peer = lax.rem(r + i, R)
            send(src_of(peer), dst, many_send.at[n], many_recv.at[n], row=peer)
            return carry

        lax.fori_loop(1, R, body, 0)

    def to_z(buf, n):
        def body(i, carry):
            send(buf.at[k, z], buf.at[k, z], many_send.at[n], many_recv.at[n], row=row_of(z + i, k))
            return carry

        lax.fori_loop(1, Z, body, 0)

    def z_to_sib(buf, n):
        got(buf.at[0, pl.ds(0, Z - 1)], many_recv.at[n])
        send(buf.at[k], buf.at[k], many_send.at[n + 1], many_recv.at[n + 1], row=row_of(z, 1 - k))

    z_step(1)
    sib_step(0)
    to_col(lambda peer: sqx.at[c], sqx.at[c], 0)
    to_z(spt, 1)

    p_in.wait()
    pslot = lax.broadcasted_iota(jnp.int32, (LP, 128), 0)
    p32 = []
    for i in range(8):
        rows = praw[i].astype(F32)
        p32.append(jnp.where(pslot < plen_ref[i], rows, rows[0:1]))
    xbuf[...] = jnp.swapaxes(jnp.stack(p32, axis=0), 0, 1).reshape(LP * 8, 128).astype(BF)

    def maxsim(b):
        s = nt(xbuf[...], qbuf[b])
        m = jnp.max(s.reshape(LP, 8, N), axis=0)
        acc = m[:, 0:128]
        for t in range(1, N // 128):
            acc = acc + m[:, 128 * t : 128 * t + 128]
        return spread(acc)

    def teach(blocks):
        found = [maxsim(b) for b in blocks]
        for b, v in zip(blocks, found):
            tblk[b] = v
            if b is r:
                town[k, z] = v
        for b in blocks:
            if b is not r:
                send(tblk.at[b], town.at[k, z], many_send.at[12], many_recv.at[12], row=b)

    def student_logits():
        got(sqx.at[pl.ds(0, C - 1)], many_recv.at[0])
        got(spt.at[1 - k], many_recv.at[2])
        part = jnp.zeros((PB, 128), F32)
        order = [PR * (2 * zz + kk) + u for kk in range(2) for zz in range(Z) for u in range(PR)]
        rhs = jnp.concatenate([sqx[i] for i in order], axis=0).astype(BF)
        aP, bP = eye(PB)
        unit = (aP == bP).astype(BF)
        for g in range(3):
            wide = spt[:, :, 8 * PR * g : 8 * PR * (g + 1), :].reshape(2 * Z * 8 * PR, PB)
            back = nt(unit, wide).astype(BF)
            part = jnp.where(lane_group == g, nn(back, rhs), part)
        sbuf[...] = SCALE * spread(part)

    rank = lax.div(rows_p, 8)
    p_index = c * PB + (2 * lax.rem(rank, Z) + lax.div(rank, Z)) * 8 + lax.rem(rows_p, 8)

    def onehot():
        wanted = jnp.zeros((1, 128), jnp.int32)
        within = lax.rem(lane, QB)
        for i in range(QB):
            wanted = jnp.where(within == i, pos_ref[i], wanted)
        return p_index == wanted

    def student_stats():
        s = sbuf[...]
        top = jnp.max(s, axis=0, keepdims=True)
        mass = jnp.sum(jnp.exp(s - top), axis=0, keepdims=True)
        hit = jnp.sum(jnp.where(onehot(), s, 0.0), axis=0, keepdims=True)
        sst[c] = jnp.where(lane_group == 0, top, jnp.where(lane_group == 1, mass, hit))
        to_col(lambda peer: sst.at[c], sst.at[c], 3)
        to_row(lambda peer: sqx.at[pl.ds(PR * peer, PR)], sqr.at[r], 4)
        sqr[r] = sqx[pl.ds(PR * r, PR)]

    def only(v, g):
        return spread(jnp.where(lane_group == g, v, 0.0))

    def pack(dst, weights, stats):
        hi, lo = split2(weights)
        u = nn(spt[...].reshape(2 * Z * DR, PB), jnp.concatenate([hi, lo], axis=1))
        u = u[:, 0:128] + u[:, 128:256]
        for kk in range(2):
            for zz in range(Z):
                for uu in range(PR):
                    base = (kk * Z + zz) * DR + 8 * uu
                    piece = stats
                    for g in range(3):
                        at = base + 8 * PR * g
                        piece = jnp.where(lane_group == g, u[at : at + 8], piece)
                    dst[PR * (2 * zz + kk) + uu] = piece

    def student_slopes():
        got(sst.at[pl.ds(0, C - 1)], many_recv.at[3])
        rows = [sst[i] for i in range(C)]
        top = only(functools.reduce(jnp.maximum, rows), 0)
        mass = jnp.zeros((1, 128), F32)
        hit = jnp.zeros((1, 128), F32)
        for v in rows:
            mass = mass + jnp.where(lane_group == 0, jnp.exp(jnp.minimum(v - top, 0.0)) * pltpu.roll(v, 96, 1), 0.0)
            hit = hit + v
        mass = spread(mass)
        hit = only(hit, 2)
        zz_ = 2.0 * (jnp.exp(sbuf[...] - top) / mass) - jnp.where(onehot(), 1.0, 0.0)
        pack(upz, zz_, jnp.zeros((8, 128), F32))
        vbuf[c] = upz[c]
        to_col(lambda peer: upz.at[peer], vbuf.at[c], 5)
        quarter = PB // GROUPS
        small = jnp.zeros((quarter, 128), F32)
        for g in range(GROUPS):
            small = jnp.where(lane_group == g, zz_[quarter * g : quarter * (g + 1)], small)
        zag[k, z] = small
        to_z(zag, 6)
        return top + jnp.log(mass), hit

    def unpack_slopes():
        got(zag.at[1 - k], many_recv.at[7])
        quarter = PB // GROUPS
        for t in range(T):
            for g in range(GROUPS):
                tile = jnp.zeros((quarter, 128), F32)
                for b in range(GROUPS):
                    rr = GROUPS * t + b
                    v = zag[rr % 2, rr // 2]
                    if b != g:
                        v = pltpu.roll(v, ((b - g) % GROUPS) * QB, 1)
                    tile = jnp.where(lane_group == b, v, tile)
                zfull[t, quarter * g : quarter * (g + 1)] = tile

    def unpack_queries():
        got(sqr.at[pl.ds(0, R - 1)], many_recv.at[4])
        tiles = []
        for t in range(T):
            rows = []
            for u in range(PR):
                for g in range(3):
                    tile = jnp.zeros((8, 128), F32)
                    for b in range(GROUPS):
                        v = sqr[GROUPS * t + b, u]
                        if b != g:
                            v = pltpu.roll(v, ((b - g) % GROUPS) * QB, 1)
                        tile = jnp.where(lane_group == b, v, tile)
                    rows.append(tile)
            tiles.append(jnp.concatenate(rows, axis=0).astype(BF))
        return tiles

    other = sib_got(0)
    teach([r, other])
    z_got(1)
    if Z // 2 > 1:
        z_step(2)
    z_to_sib(spt, 1)
    first = [j for j in range(len(offsets)) if abs(offsets[j]) == 1]
    for j in first:
        xy_step(j)
    student_logits()
    student_stats()
    kept = None
    for s in range(1, Z // 2 + 1):
        js = [j for j in range(len(offsets)) if abs(offsets[j]) == s]
        for j in js:
            xy_got(j)
            sib_step(j + 1)
        if s < Z // 2:
            z_got(s + 1)
            if s + 1 < Z // 2:
                z_step(s + 2)
            for j in range(len(offsets)):
                if abs(offsets[j]) == s + 1:
                    xy_step(j)
        if s < Z // 2:
            teach([row_of(z + offsets[j], k) for j in js])
            if s == 1:
                kept = student_slopes()
            if s == 2:
                z_to_sib(zag, 6)
            teach([sib_got(j + 1) for j in js])
        else:
            if kept is None:
                kept = student_slopes()
            if s <= 2:
                z_to_sib(zag, 6)
            unpack_slopes()
            teach([row_of(z + offsets[js[0]], k), sib_got(js[0] + 1)])
    student_lse, hit = kept

    for t in range(T):
        tile = tblk[GROUPS * t]
        for b in range(1, GROUPS):
            tile = jnp.where(lane_group == b, tblk[GROUPS * t + b], tile)
        tag[k, z, t] = tile
    to_z(tag, 8)
    got(tblk.at[pl.ds(0, R - 1)], many_recv.at[12])
    t_own = town[...].reshape(PB, 128)
    top = jnp.max(t_own, axis=0, keepdims=True)
    e = jnp.exp(t_own - top)
    mass = jnp.sum(e, axis=0, keepdims=True)
    cross = jnp.sum(e * (t_own - sbuf[...]), axis=0, keepdims=True)
    row8 = lax.broadcasted_iota(jnp.int32, (8, 128), 0)
    pack(upt, e, jnp.where(row8 == 0, top, jnp.where(row8 == 1, mass, cross)))
    ubuf[c] = upt[c]
    to_col(lambda peer: upt.at[peer], ubuf.at[c], 10)
    z_to_sib(tag, 8)
    sq_tiles = unpack_queries()
    got(vbuf.at[pl.ds(0, C - 1)], many_recv.at[5])
    v_sum = functools.reduce(jnp.add, [vbuf[i] for i in range(C)])

    got(ubuf.at[pl.ds(0, C - 1)], many_recv.at[10])
    highest = functools.reduce(jnp.maximum, [ubuf[i] for i in range(C)])
    top = only(highest, 3)[0:1]
    acc = jnp.zeros((8, 128), F32)
    for i in range(C):
        v = ubuf[i]
        w = only(jnp.exp(jnp.minimum(v[0:1] - top, 0.0)), 3)
        acc = acc + w * v
    whole = only(acc, 3)
    mass, cross = whole[1:2], whole[2:3]
    inverse = 1.0 / mass
    qg_ref[...] = (SCALE / total) * (v_sum - acc * inverse)
    per_query = cross * inverse - (top + jnp.log(mass)) + 2.0 * student_lse - hit
    fin[r] = jnp.where(lane_group == 0, top, jnp.where(lane_group == 1, inverse, per_query))
    to_row(lambda peer: fin.at[r], fin.at[r], 11)
    got(tag.at[1 - k], many_recv.at[9])

    got(fin.at[pl.ds(0, R - 1)], many_recv.at[11])
    grads = jnp.zeros((PB, DR), F32)
    per_query = jnp.zeros((1, 128), F32)
    for t in range(T):
        tops = jnp.zeros((1, 128), F32)
        inverses = jnp.zeros((1, 128), F32)
        for b in range(GROUPS):
            v = fin[GROUPS * t + b]
            per_query = per_query + jnp.where(lane_group == 2, v, 0.0)
            tops = jnp.where(lane_group == b, pltpu.roll(v, b * QB, 1) if b else v, tops)
            inverses = jnp.where(lane_group == b, pltpu.roll(v, ((b - 1) % GROUPS) * QB, 1) if b != 1 else v, inverses)
        probs = jnp.exp(tag[:, :, t].reshape(PB, 128) - tops) * inverses
        hi, lo = split2(zfull[t] - probs)
        grads = grads + nt(hi, sq_tiles[t]) + nt(lo, sq_tiles[t])
    grads = grads * (SCALE / total)
    for kk in range(2):
        for zz in range(Z):
            pg_ref[8 * (2 * zz + kk) : 8 * (2 * zz + kk) + 8, :] = grads[8 * (kk * Z + zz) : 8 * (kk * Z + zz) + 8]
    loss_ref[...] = jnp.zeros((1, 128), F32) + jnp.sum(per_query) / total

    for s in range(1, Z // 2 + 1):
        last = s == Z // 2
        a, b = (mine_a, mine_b) if last else (mine, mine)
        left(qbuf.at[row_of(z - (s - 1), k), a], z_send.at[0, s - 1])
        left(qbuf.at[row_of(z + (s - 1), k), b], z_send.at[1, s - 1])
    for j in range(len(offsets)):
        b = row_of(z + offsets[j], k)
        for n, part in enumerate((mine, mine, mine_a, mine_b)):
            left(qbuf.at[b, part], xy_send.at[n, j])
    for j in range(len(offsets) + 1):
        left(qbuf.at[r], sib_send.at[j])
    for n, buf, count in ((0, sqx, C), (3, sst, C), (5, upz, C), (10, upt, C), (4, sqr, R), (11, fin, R), (12, tblk, R)):
        left(buf.at[pl.ds(0, count - 1)], many_send.at[n])
    for n, buf in ((1, spt), (6, zag), (8, tag)):
        left(buf.at[0, pl.ds(0, Z - 1)], many_send.at[n])
        left(buf.at[0], many_send.at[n + 1])


def shards(query_tokens, query_lengths, passage_tokens, passage_lengths, student_queries, student_passages, positives):
    R = lax.axis_size("row")
    C = lax.axis_size("col")
    Z = R // 2
    L = query_tokens.shape[1]
    LP = passage_tokens.shape[1]
    PB = 8 * R
    PR = C // R
    DR = student_passages.shape[1]
    T = R // GROUPS
    hops = Z - 1
    dma = pltpu.SemaphoreType.DMA
    vmem = pl.BlockSpec(memory_space=pltpu.VMEM)
    smem = pl.BlockSpec(memory_space=pltpu.SMEM)
    anywhere = pl.BlockSpec(memory_space=pl.ANY)
    pg, qg, loss = pl.pallas_call(
        functools.partial(kernel, R, C),
        out_shape=(
            jax.ShapeDtypeStruct((PB, DR), F32),
            jax.ShapeDtypeStruct((8, 128), F32),
            jax.ShapeDtypeStruct((1, 128), F32),
        ),
        in_specs=[anywhere, smem, anywhere, smem, vmem, vmem, smem],
        out_specs=(vmem, vmem, vmem),
        scratch_shapes=[
            pltpu.VMEM((QB, L, 128), BF),
            pltpu.VMEM((8, LP, 128), BF),
            pltpu.VMEM((R, QB * L, 128), BF),
            pltpu.VMEM((LP * 8, 128), BF),
            pltpu.VMEM((C, 8, 128), F32),
            pltpu.VMEM((2, Z, DR, PB), BF),
            pltpu.VMEM((C, 1, 128), F32),
            pltpu.VMEM((PB, 128), F32),
            pltpu.VMEM((C, 8, 128), F32),
            pltpu.VMEM((C, 8, 128), F32),
            pltpu.VMEM((2, Z, PB // GROUPS, 128), F32),
            pltpu.VMEM((T, PB, 128), F32),
            pltpu.VMEM((R, PR, 8, 128), F32),
            pltpu.VMEM((R, 8, 128), F32),
            pltpu.VMEM((2, Z, 8, 128), F32),
            pltpu.VMEM((2, Z, T, 8, 128), F32),
            pltpu.VMEM((C, 8, 128), F32),
            pltpu.VMEM((C, 8, 128), F32),
            pltpu.VMEM((R, 1, 128), F32),
            dma((2,)),
            dma((2, Z // 2)),
            dma((2, Z // 2)),
            dma((4, hops)),
            dma((4, hops)),
            dma((hops + 1,)),
            dma((hops + 1,)),
            dma((13,)),
            dma((13,)),
        ],
        compiler_params=pltpu.CompilerParams(
            collective_id=0, has_side_effects=True, vmem_limit_bytes=48 * 1024 * 1024
        ),
        name="distill",
    )(query_tokens, query_lengths, passage_tokens, passage_lengths, student_queries, student_passages, positives)
    qg = qg.reshape(8, GROUPS, QB)[:, :3].transpose(2, 1, 0).reshape(QB, 24)
    return qg, pg, loss[0, 0]


def solution(mesh):
    return jax.shard_map(
        shards,
        mesh=mesh,
        in_specs=(
            P("row", None, None),
            P("row"),
            P(("col", "row"), None, None),
            P(("col", "row")),
            P("row", "col"),
            P("col", "row"),
            P("row"),
        ),
        out_specs=(P("row", "col"), P("col", "row"), P()),
        check_vma=False,
    )
```

time: 528 us -> 72.4 us (0.14)
  blocking collectives: 250 us -> 0 us
  waiting for transfers between devices: 234 us -> 0 us
  Pallas kernels: 0 us -> 65.6 us
  matrix products: 20.2 us -> 0 us
  between operations: 15.2 us -> 1.84 us
    unnamed x4 -> x0, waiting for transfers between devices: 169 us -> none
    psum x2 -> x0, blocking collectives: 108 us -> none  [the longest x1 56.2 us: shards(): lax.psum((jnp.sum(teacher_exp, axis=1), jnp.sum(student_exp, axis=1), jnp...]
    all_gather x2 -> x0, blocking collectives: 66.8 us -> none  [the longest x1 41.1 us: shards(): full_queries = lax.all_gather(student_queries, 'col', axis=1, tiled=True)]
    pallas_call x0 -> x1, Pallas kernels: none -> 65.6 us  [shards(): pl.pallas_call(functools.partial(kernel, R, C), out_shape=(jax.ShapeDtype...]
    reduce_scatter x1 -> x0, waiting for transfers between devices: 64.7 us -> none  [shards(): lax.psum_scatter(passage_terms, 'row', scatter_dimension=1, tiled=True)]
    pmax x1 -> x0, blocking collectives: 57.1 us -> none  [shards(): lax.pmax((local_teacher_max, local_student_max), 'col')]
    dot_general x14 -> x0, matrix products: 20.2 us -> none  [the longest x11 17.6 us: token_block_max(): jnp.einsum('ie,pte->itp', query_rows, block, preferred_element_type=jnp.f...]
    unnamed x1 -> x0, blocking collectives: 17.9 us -> none
  transfers between devices with their start and end apart: 3 -> 0, of which waited for: 2 -> 0; matrix products, arithmetic and copies ran while one was open for 1% -> 0% of each run, Pallas kernels for 0% -> 0%
where the time goes in v1:
time: 72.4 us; the launch traced here: 72.2 us
  Pallas kernels  65.6 us (91%)
  local copies, waits for them, and re-layouts  4.76 us (7%)
  between operations  1.84 us (3%)
    pallas_call x1, Pallas kernels, shards(): pl.pallas_call(functools.partial(kernel, R, C), out_shape=(jax.ShapeDtype...  65.6 us
    unnamed x15, local copies, waits for them, and re-layouts  4.07 us

profile of v1, /device:TPU:1, one launch (start us, length us, event | category | flops | bytes accessed | tf_op | source)
XLA Modules:
  0.0 72.2 jit_solution(16258402242962745980)
XLA Ops:
  0.6 0.0 copy-start.5
  0.6 0.8 %copy.10.sq_ref = bf16[32,24]{1,0:T(8,128)(2,1)S(1)} copy(bf16[32,24]{0,1:T(8,128)(2,1)} %param.11) | data formatting | bytes 3072 | tf_op args[4]
  1.4 0.0 copy-done.5
  1.4 0.0 copy-start.2
  1.4 0.0 copy-start.3
  1.4 0.0 copy-start.4
  1.4 0.1 copy.11.sp_ref
  1.6 0.5 copy-done.2
  2.1 0.0 copy-done.3
  2.1 0.0 copy-done.4
  2.1 0.0 copy-start
  2.1 1.0 %copy-done = bf16[8,176,128]{2,1,0:T(8,128)(2,1)S(1)} copy-done((bf16[8,176,128]{2,1,0:T(8,128)(2,1)S(1)}, bf16[8,176,128]{2,1,0:T(8,128)(2,1)}, u32[]{:S(2)}) %copy-start) | copy-done | bytes 360472
  3.1 0.0 copy-start.1
  3.1 0.9 %copy-done.1 = bf16[32,32,128]{2,1,0:T(8,128)(2,1)S(1)} copy-done((bf16[32,32,128]{2,1,0:T(8,128)(2,1)S(1)}, bf16[32,32,128]{2,1,0:T(8,128)(2,1)}, u32[]{:S(2)}) %copy-start.1) | copy-done | bytes 262168
  4.0 65.6 %distill.1 = (f32[128,48]{1,0:T(8,128)S(1)}, f32[8,128]{1,0:T(8,128)S(1)}, f32[1,128]{1,0:T(1,128)S(1)}) custom-call(bf16[32,32,128]{2,1,0:T(8,128)(2,1)S(1)} %copy-done.1, s32[32]{0:T(128)S(1)} %copy-done.2, bf16[8,176,128]{2,1,0:T(8,128)(2,1)S(1)} %copy-done, s32[8]{0:T(128)S(1)} %copy-done.3, bf16[32,24]{1,0:T(8,128)(2,1)S(1)} %copy.10.sq_ref, ...), custom_call_target="tpu_custom_call" | custom-call | tf_op jit(solution)/shard_map/distill/pallas_call | solution.py:519
  69.6 0.1 reshape.12
  69.7 0.6 copy.15
  70.3 0.7 copy.13
  (1 shorter events, 0.0 us)
Async XLA Ops:
  0.6 0.8 %copy-start.5 = (bf16[128,48]{0,1:T(8,128)(2,1)S(1)}, bf16[128,48]{0,1:T(8,128)(2,1)}, u32[]{:S(2)}) copy-start(bf16[128,48]{0,1:T(8,128)(2,1)} %param.12) | copy-start | bytes 36868
  1.4 0.7 copy-start.2
  1.4 0.7 copy-start.3
  1.4 0.7 copy-start.4
  2.1 1.0 %copy-start = (bf16[8,176,128]{2,1,0:T(8,128)(2,1)S(1)}, bf16[8,176,128]{2,1,0:T(8,128)(2,1)}, u32[]{:S(2)}) copy-start(bf16[8,176,128]{2,1,0:T(8,128)(2,1)} %pt_ref.1) | copy-start | bytes 1081348
  3.1 0.9 %copy-start.1 = (bf16[32,32,128]{2,1,0:T(8,128)(2,1)S(1)}, bf16[32,32,128]{2,1,0:T(8,128)(2,1)}, u32[]{:S(2)}) copy-start(bf16[32,32,128]{2,1,0:T(8,128)(2,1)} %qt_ref.1) | copy-start | bytes 786436

commit v2 on v1

--- a/solution.py
+++ b/solution.py
@@ -37,16 +37,21 @@
 def kernel(
     R,
     C,
-    qt_ref,
-    qlen_ref,
-    pt_ref,
-    plen_ref,
-    sq_ref,
-    sp_ref,
-    pos_ref,
+    qt_hbm,
+    qlen_hbm,
+    pt_hbm,
+    plen_hbm,
+    sq_hbm,
+    sp_hbm,
+    pos_hbm,
     pg_ref,
     qg_ref,
     loss_ref,
+    qlen_ref,
+    plen_ref,
+    pos_ref,
+    sq_ref,
+    sp_ref,
     qraw,
     praw,
     qbuf,
@@ -79,8 +84,8 @@
     Z = R // 2
     XC = min(X_CHIPS, C)
     YC = C // XC
-    L = qt_ref.shape[1]
-    LP = pt_ref.shape[1]
+    L = qt_hbm.shape[1]
+    LP = pt_hbm.shape[1]
     N = QB * L
     SL = N // 4
     HALF = SL // 2
@@ -119,10 +124,6 @@
             src_ref=src, dst_ref=src, send_sem=s_sem, recv_sem=s_sem, device_id={"row": r}, device_id_type=MESH
         ).wait_send()
 
-    q_in = pltpu.make_async_copy(qt_ref, qraw, in_sem.at[0])
-    p_in = pltpu.make_async_copy(pt_ref, praw, in_sem.at[1])
-    q_in.start()
-    p_in.start()
     barrier = pltpu.get_barrier_semaphore()
 
     def greet_col(i, carry):
@@ -133,38 +134,85 @@
         pl.semaphore_signal(barrier, inc=1, device_id={"row": lax.rem(r + i, R)}, device_id_type=MESH)
         return carry
 
+    inputs = [
+        pltpu.make_async_copy(src, dst, in_sem.at[n])
+        for n, (src, dst) in enumerate(
+            (
+                (qt_hbm, qraw),
+                (qlen_hbm, qlen_ref),
+                (pt_hbm, praw),
+                (plen_hbm, plen_ref),
+                (sq_hbm, sq_ref),
+                (sp_hbm, sp_ref),
+                (pos_hbm, pos_ref),
+            )
+        )
+    ]
+    for copy in inputs:
+        copy.start()
+    lax.fori_loop(1, R, greet_row, 0)
     lax.fori_loop(1, C, greet_col, 0)
-    lax.fori_loop(1, R, greet_row, 0)
 
     rows_p = lax.broadcasted_iota(jnp.int32, (PB, 128), 0)
     lane = lax.broadcasted_iota(jnp.int32, (1, 128), 1)
     lane_group = lax.div(lane, QB)
 
-    def eye(n):
-        a = lax.broadcasted_iota(jnp.int32, (n, n), 0)
-        b = lax.broadcasted_iota(jnp.int32, (n, n), 1)
-        return a, b
-
-    a24, b24 = eye(24)
-    sq_t = nt((a24 == b24).astype(BF), jnp.concatenate([sq_ref[...]] * GROUPS, axis=0))
-    packed = jnp.zeros((8, 128), F32)
-    for g in range(3):
-        packed = jnp.where(lane_group == g, sq_t[8 * g : 8 * g + 8], packed)
-    sqx[c] = packed
-    aD, bD = eye(DR)
-    source = lax.rem(lax.div(aD, 8), PR) * 24 + lax.div(aD, 8 * PR) * 8 + lax.rem(aD, 8)
-    sp32 = sp_ref[...].astype(F32)
-    sp_perm = jnp.concatenate(
-        [sp32[8 * (2 * zz + kk) : 8 * (2 * zz + kk) + 8] for kk in range(2) for zz in range(Z)], axis=0
-    ).astype(BF)
-    spt[k, z] = nt((source == bD).astype(BF), sp_perm).astype(BF)
-
-    q_in.wait()
+    def natural(i):
+        rank = lax.div(i, 8)
+        return (2 * lax.rem(rank, Z) + lax.div(rank, Z)) * 8 + lax.rem(i, 8)
+
+    inputs[0].wait()
+    inputs[1].wait()
     slot = lax.broadcasted_iota(jnp.int32, (L, 128), 0)
     q32 = jnp.stack(
         [jnp.where(slot < qlen_ref[i], qraw[i].astype(F32), 0.0) for i in range(QB)], axis=0
     )
     qbuf[r] = jnp.swapaxes(q32, 0, 1).reshape(N, 128).astype(BF)
+
+    inputs[4].wait()
+    inputs[5].wait()
+    qa = lax.broadcasted_iota(jnp.int32, (QB, 128), 0)
+    qb = lax.broadcasted_iota(jnp.int32, (QB, 128), 1)
+    sq_wide = nn(sq_ref[...], (qa == lax.rem(qb, QB)).astype(BF))
+    packed = jnp.zeros((8, 128), F32)
+    for g in range(3):
+        packed = jnp.where(lane_group == g, sq_wide[8 * g : 8 * g + 8], packed)
+    sqx[c] = packed
+    pa = lax.broadcasted_iota(jnp.int32, (PB, PB), 0)
+    pb = lax.broadcasted_iota(jnp.int32, (PB, PB), 1)
+    sp_wide = nn(sp_ref[...], (pa == natural(pb)).astype(BF))
+    spt[k, z] = jnp.concatenate(
+        [sp_wide[24 * u + 8 * g : 24 * u + 8 * g + 8] for g in range(3) for u in range(PR)], axis=0
+    ).astype(BF)
+
+    inputs[2].wait()
+    inputs[3].wait()
+    inputs[6].wait()
+    pslot = lax.broadcasted_iota(jnp.int32, (LP, 128), 0)
+    p32 = []
+    for i in range(8):
+        rows = praw[i].astype(F32)
+        p32.append(jnp.where(pslot < plen_ref[i], rows, rows[0:1]))
+    xbuf[...] = jnp.swapaxes(jnp.stack(p32, axis=0), 0, 1).reshape(LP * 8, 128).astype(BF)
+
+    def maxsim(b):
+        s = nt(xbuf[...], qbuf[b])
+        m = jnp.max(s.reshape(LP, 8, N), axis=0)
+        acc = m[:, 0:128]
+        for t in range(1, N // 128):
+            acc = acc + m[:, 128 * t : 128 * t + 128]
+        return spread(acc)
+
+    def teach(blocks):
+        found = [maxsim(b) for b in blocks]
+        for b, v in zip(blocks, found):
+            tblk[b] = v
+        for b in blocks:
+            send(tblk.at[b], town.at[k, z], many_send.at[12], many_recv.at[12], row=b)
+
+    own = maxsim(r)
+    tblk[r] = own
+    town[k, z] = own
 
     pl.semaphore_wait(barrier, C - 1 + R - 1)
 
@@ -254,48 +302,20 @@
     to_col(lambda peer: sqx.at[c], sqx.at[c], 0)
     to_z(spt, 1)
 
-    p_in.wait()
-    pslot = lax.broadcasted_iota(jnp.int32, (LP, 128), 0)
-    p32 = []
-    for i in range(8):
-        rows = praw[i].astype(F32)
-        p32.append(jnp.where(pslot < plen_ref[i], rows, rows[0:1]))
-    xbuf[...] = jnp.swapaxes(jnp.stack(p32, axis=0), 0, 1).reshape(LP * 8, 128).astype(BF)
-
-    def maxsim(b):
-        s = nt(xbuf[...], qbuf[b])
-        m = jnp.max(s.reshape(LP, 8, N), axis=0)
-        acc = m[:, 0:128]
-        for t in range(1, N // 128):
-            acc = acc + m[:, 128 * t : 128 * t + 128]
-        return spread(acc)
-
-    def teach(blocks):
-        found = [maxsim(b) for b in blocks]
-        for b, v in zip(blocks, found):
-            tblk[b] = v
-            if b is r:
-                town[k, z] = v
-        for b in blocks:
-            if b is not r:
-                send(tblk.at[b], town.at[k, z], many_send.at[12], many_recv.at[12], row=b)
-
     def student_logits():
         got(sqx.at[pl.ds(0, C - 1)], many_recv.at[0])
         got(spt.at[1 - k], many_recv.at[2])
         part = jnp.zeros((PB, 128), F32)
         order = [PR * (2 * zz + kk) + u for kk in range(2) for zz in range(Z) for u in range(PR)]
         rhs = jnp.concatenate([sqx[i] for i in order], axis=0).astype(BF)
-        aP, bP = eye(PB)
-        unit = (aP == bP).astype(BF)
+        unit = (pa == pb).astype(BF)
         for g in range(3):
             wide = spt[:, :, 8 * PR * g : 8 * PR * (g + 1), :].reshape(2 * Z * 8 * PR, PB)
             back = nt(unit, wide).astype(BF)
             part = jnp.where(lane_group == g, nn(back, rhs), part)
         sbuf[...] = SCALE * spread(part)
 
-    rank = lax.div(rows_p, 8)
-    p_index = c * PB + (2 * lax.rem(rank, Z) + lax.div(rank, Z)) * 8 + lax.rem(rows_p, 8)
+    p_index = c * PB + natural(rows_p)
 
     def onehot():
         wanted = jnp.zeros((1, 128), jnp.int32)
@@ -319,8 +339,8 @@
 
     def pack(dst, weights, stats):
         hi, lo = split2(weights)
-        u = nn(spt[...].reshape(2 * Z * DR, PB), jnp.concatenate([hi, lo], axis=1))
-        u = u[:, 0:128] + u[:, 128:256]
+        table = spt[...].reshape(2 * Z * DR, PB)
+        u = nn(jnp.concatenate([table, table], axis=1), jnp.concatenate([hi, lo], axis=0))
         for kk in range(2):
             for zz in range(Z):
                 for uu in range(PR):
@@ -385,45 +405,60 @@
             tiles.append(jnp.concatenate(rows, axis=0).astype(BF))
         return tiles
 
-    other = sib_got(0)
-    teach([r, other])
-    z_got(1)
-    if Z // 2 > 1:
-        z_step(2)
-    z_to_sib(spt, 1)
-    first = [j for j in range(len(offsets)) if abs(offsets[j]) == 1]
-    for j in first:
-        xy_step(j)
-    student_logits()
-    student_stats()
-    kept = None
-    for s in range(1, Z // 2 + 1):
-        js = [j for j in range(len(offsets)) if abs(offsets[j]) == s]
-        for j in js:
+    half = Z // 2
+
+    def at(s, kk):
+        return [row_of(z + o, kk) for o in offsets if abs(o) == s]
+
+    def numbers(s):
+        return [j for j, o in enumerate(offsets) if abs(o) == s]
+
+    def z_turn(s):
+        z_got(s)
+        if s < half:
+            z_step(s + 1)
+        for j in numbers(s):
+            xy_step(j)
+
+    def whole(s):
+        for j in numbers(s):
             xy_got(j)
             sib_step(j + 1)
-        if s < Z // 2:
-            z_got(s + 1)
-            if s + 1 < Z // 2:
-                z_step(s + 2)
-            for j in range(len(offsets)):
-                if abs(offsets[j]) == s + 1:
-                    xy_step(j)
-        if s < Z // 2:
-            teach([row_of(z + offsets[j], k) for j in js])
-            if s == 1:
-                kept = student_slopes()
-            if s == 2:
-                z_to_sib(zag, 6)
-            teach([sib_got(j + 1) for j in js])
-        else:
-            if kept is None:
-                kept = student_slopes()
-            if s <= 2:
-                z_to_sib(zag, 6)
-            unpack_slopes()
-            teach([row_of(z + offsets[js[0]], k), sib_got(js[0] + 1)])
-    student_lse, hit = kept
+
+    def handed(s):
+        for j in numbers(s):
+            sib_got(j + 1)
+
+    teach([sib_got(0)])
+    z_turn(1)
+    z_to_sib(spt, 1)
+    if half >= 2:
+        z_turn(2)
+    whole(1)
+    if half >= 2:
+        teach(at(1, k))
+        if half >= 3:
+            z_turn(3)
+        student_logits()
+        student_stats()
+        for s in range(2, half + 1):
+            whole(s)
+            if s + 2 <= half:
+                z_turn(s + 2)
+            if s < half:
+                teach(at(s, k))
+                handed(s)
+                teach(at(s, 1 - k))
+            else:
+                handed(s)
+                teach(at(s, k) + at(s, 1 - k))
+        handed(1)
+        teach(at(1, 1 - k))
+    else:
+        student_logits()
+        student_stats()
+        handed(1)
+        teach(at(1, k) + at(1, 1 - k))
 
     for t in range(T):
         tile = tblk[GROUPS * t]
@@ -431,6 +466,7 @@
             tile = jnp.where(lane_group == b, tblk[GROUPS * t + b], tile)
         tag[k, z, t] = tile
     to_z(tag, 8)
+    student_lse, hit = student_slopes()
     got(tblk.at[pl.ds(0, R - 1)], many_recv.at[12])
     t_own = town[...].reshape(PB, 128)
     top = jnp.max(t_own, axis=0, keepdims=True)
@@ -441,30 +477,33 @@
     pack(upt, e, jnp.where(row8 == 0, top, jnp.where(row8 == 1, mass, cross)))
     ubuf[c] = upt[c]
     to_col(lambda peer: upt.at[peer], ubuf.at[c], 10)
-    z_to_sib(tag, 8)
+    z_to_sib(zag, 6)
     sq_tiles = unpack_queries()
     got(vbuf.at[pl.ds(0, C - 1)], many_recv.at[5])
     v_sum = functools.reduce(jnp.add, [vbuf[i] for i in range(C)])
 
     got(ubuf.at[pl.ds(0, C - 1)], many_recv.at[10])
-    highest = functools.reduce(jnp.maximum, [ubuf[i] for i in range(C)])
-    top = only(highest, 3)[0:1]
+    tops = only(jnp.concatenate([ubuf[i, 0:1] for i in range(C)], axis=0), 3)
+    top = jnp.max(tops, axis=0, keepdims=True)
+    weights = jnp.exp(tops - top)
     acc = jnp.zeros((8, 128), F32)
     for i in range(C):
-        v = ubuf[i]
-        w = only(jnp.exp(jnp.minimum(v[0:1] - top, 0.0)), 3)
-        acc = acc + w * v
+        acc = acc + weights[i : i + 1] * ubuf[i]
     whole = only(acc, 3)
     mass, cross = whole[1:2], whole[2:3]
     inverse = 1.0 / mass
-    qg_ref[...] = (SCALE / total) * (v_sum - acc * inverse)
+    grads = (SCALE / total) * (v_sum - acc * inverse)
+    for g in range(3):
+        qg_ref[8 * g : 8 * g + 8, :] = (pltpu.roll(grads, 128 - QB * g, 1) if g else grads)[:, 0:QB]
     per_query = cross * inverse - (top + jnp.log(mass)) + 2.0 * student_lse - hit
     fin[r] = jnp.where(lane_group == 0, top, jnp.where(lane_group == 1, inverse, per_query))
     to_row(lambda peer: fin.at[r], fin.at[r], 11)
+    z_to_sib(tag, 8)
+    unpack_slopes()
     got(tag.at[1 - k], many_recv.at[9])
 
     got(fin.at[pl.ds(0, R - 1)], many_recv.at[11])
-    grads = jnp.zeros((PB, DR), F32)
+    grads = jnp.zeros((DR, PB), F32)
     per_query = jnp.zeros((1, 128), F32)
     for t in range(T):
         tops = jnp.zeros((1, 128), F32)
@@ -474,14 +513,14 @@
             per_query = per_query + jnp.where(lane_group == 2, v, 0.0)
             tops = jnp.where(lane_group == b, pltpu.roll(v, b * QB, 1) if b else v, tops)
             inverses = jnp.where(lane_group == b, pltpu.roll(v, ((b - 1) % GROUPS) * QB, 1) if b != 1 else v, inverses)
-        probs = jnp.exp(tag[:, :, t].reshape(PB, 128) - tops) * inverses
-        hi, lo = split2(zfull[t] - probs)
-        grads = grads + nt(hi, sq_tiles[t]) + nt(lo, sq_tiles[t])
-    grads = grads * (SCALE / total)
-    for kk in range(2):
-        for zz in range(Z):
-            pg_ref[8 * (2 * zz + kk) : 8 * (2 * zz + kk) + 8, :] = grads[8 * (kk * Z + zz) : 8 * (kk * Z + zz) + 8]
-    loss_ref[...] = jnp.zeros((1, 128), F32) + jnp.sum(per_query) / total
+        slopes = zfull[t] - jnp.exp(tag[:, :, t].reshape(PB, 128) - tops) * inverses
+        slopes = jnp.concatenate(
+            [slopes[8 * (kk * Z + zz) : 8 * (kk * Z + zz) + 8] for zz in range(Z) for kk in range(2)], axis=0
+        )
+        hi, lo = split2(slopes)
+        grads = grads + nt(jnp.concatenate([sq_tiles[t]] * 2, axis=1), jnp.concatenate([hi, lo], axis=1))
+    pg_ref[...] = grads * (SCALE / total)
+    loss_ref[...] = jnp.zeros((1, 1), F32) + jnp.sum(per_query) / total
 
     for s in range(1, Z // 2 + 1):
         last = s == Z // 2
@@ -514,18 +553,22 @@
     hops = Z - 1
     dma = pltpu.SemaphoreType.DMA
     vmem = pl.BlockSpec(memory_space=pltpu.VMEM)
-    smem = pl.BlockSpec(memory_space=pltpu.SMEM)
-    anywhere = pl.BlockSpec(memory_space=pl.ANY)
+    hbm = pl.BlockSpec(memory_space=pltpu.HBM)
     pg, qg, loss = pl.pallas_call(
         functools.partial(kernel, R, C),
         out_shape=(
-            jax.ShapeDtypeStruct((PB, DR), F32),
-            jax.ShapeDtypeStruct((8, 128), F32),
-            jax.ShapeDtypeStruct((1, 128), F32),
+            jax.ShapeDtypeStruct((DR, PB), F32),
+            jax.ShapeDtypeStruct((24, QB), F32),
+            jax.ShapeDtypeStruct((1, 1), F32),
         ),
-        in_specs=[anywhere, smem, anywhere, smem, vmem, vmem, smem],
+        in_specs=[hbm] * 7,
         out_specs=(vmem, vmem, vmem),
         scratch_shapes=[
+            pltpu.SMEM((QB,), jnp.int32),
+            pltpu.SMEM((8,), jnp.int32),
+            pltpu.SMEM((QB,), jnp.int32),
+            pltpu.VMEM((24, QB), BF),
+            pltpu.VMEM((DR, PB), BF),
             pltpu.VMEM((QB, L, 128), BF),
             pltpu.VMEM((8, LP, 128), BF),
             pltpu.VMEM((R, QB * L, 128), BF),
@@ -545,7 +588,7 @@
             pltpu.VMEM((C, 8, 128), F32),
             pltpu.VMEM((C, 8, 128), F32),
             pltpu.VMEM((R, 1, 128), F32),
-            dma((2,)),
+            dma((7,)),
             dma((2, Z // 2)),
             dma((2, Z // 2)),
             dma((4, hops)),
@@ -556,12 +599,11 @@
             dma((13,)),
         ],
         compiler_params=pltpu.CompilerParams(
-            collective_id=0, has_side_effects=True, vmem_limit_bytes=48 * 1024 * 1024
+            collective_id=0, has_side_effects=True, vmem_limit_bytes=64 * 1024 * 1024
         ),
         name="distill",
-    )(query_tokens, query_lengths, passage_tokens, passage_lengths, student_queries, student_passages, positives)
-    qg = qg.reshape(8, GROUPS, QB)[:, :3].transpose(2, 1, 0).reshape(QB, 24)
-    return qg, pg, loss[0, 0]
+    )(query_tokens, query_lengths, passage_tokens, passage_lengths, student_queries.T, student_passages.T, positives)
+    return qg.T, pg.T, loss.reshape(())
 
 
 def solution(mesh):

time: 72.4 us -> 68.6 us (0.948)
  local copies, waits for them, and re-layouts: 4.76 us -> 1.92 us
  Pallas kernels: 65.6 us -> 64 us
    unnamed x15 -> x4, local copies, waits for them, and re-layouts: 4.07 us -> 1.92 us
    pallas_call x1, Pallas kernels: 65.6 us -> 64 us  [shards(): pl.pallas_call(functools.partial(kernel, R, C), out_shape=(jax.ShapeDtype...]
where the time goes in v2:
time: 68.6 us; the launch traced here: 68.4 us
  Pallas kernels  64 us (93%)
  between operations  2.4 us (3%)
  local copies, waits for them, and re-layouts  1.92 us (3%)
    pallas_call x1, Pallas kernels, shards(): pl.pallas_call(functools.partial(kernel, R, C), out_shape=(jax.ShapeDtype...  64 us
    unnamed x4, local copies, waits for them, and re-layouts  1.92 us

profile of v2, /device:TPU:1, one launch (start us, length us, event | category | flops | bytes accessed | tf_op | source)
XLA Modules:
  0.0 68.4 jit_solution(10998696482407208160)
XLA Ops:
  0.6 64.0 %distill.1 = (f32[48,128]{1,0:T(8,128)}, f32[24,32]{1,0:T(8,128)}, f32[1,1]{1,0:T(1,128)}) custom-call(bf16[32,32,128]{2,1,0:T(8,128)(2,1)} %qt_hbm.1, s32[32]{0:T(128)} %qlen_hbm.1, bf16[8,176,128]{2,1,0:T(8,128)(2,1)} %pt_hbm.1, s32[8]{0:T(128)} %plen_hbm.1, bf16[24,32]{1,0:T(8,128)(2,1)} %bitcast.8, bf16[48,128]{1,0:T(8,128)(2,1)} %bitcast.7, s32[32]{0:T(128)} %pos_hbm.1), custom_call_target="tpu_custom_call" | custom-call | tf_op jit(solution)/shard_map/distill/pallas_call | solution.py:557
  64.7 0.0 copy-start
  64.7 1.3 %copy.13 = f32[32,24]{0,1:T(8,128)} copy(f32[32,24]{0,1:T(8,128)} %bitcast.6) | data formatting | bytes 6144
  66.0 0.0 copy-done
  66.0 0.6 copy.14
Async XLA Ops:
  64.7 1.3 %copy-start = (f32[48,128]{1,0:T(8,128)S(1)}, f32[48,128]{1,0:T(8,128)}, u32[]{:S(2)}) copy-start(f32[48,128]{1,0:T(8,128)} %get-tuple-element.7) | copy-start | bytes 73732

commit v3 on v2

--- a/solution.py
+++ b/solution.py
@@ -74,6 +74,12 @@
     in_sem,
     z_send,
     z_recv,
+    s_send,
+    s_recv,
+    x_send,
+    x_recv,
+    y_send,
+    y_recv,
     xy_send,
     xy_recv,
     sib_send,
@@ -126,13 +132,17 @@
 
     barrier = pltpu.get_barrier_semaphore()
 
-    def greet_col(i, carry):
-        pl.semaphore_signal(barrier, inc=1, device_id={"col": lax.rem(c + i, C)}, device_id_type=MESH)
-        return carry
-
-    def greet_row(i, carry):
-        pl.semaphore_signal(barrier, inc=1, device_id={"row": lax.rem(r + i, R)}, device_id_type=MESH)
-        return carry
+    neighbours = (
+        {"row": row_of(z, 1 - k)},
+        {"row": row_of(z + 1, k)},
+        {"row": row_of(z - 1, k)},
+        {"col": col_of(x + 1, y)},
+        {"col": col_of(x - 1, y)},
+        {"col": col_of(x, y + 1)},
+        {"col": col_of(x, y - 1)},
+    )
+    for peer in neighbours:
+        pl.semaphore_signal(barrier, inc=1, device_id=peer, device_id_type=MESH)
 
     inputs = [
         pltpu.make_async_copy(src, dst, in_sem.at[n])
@@ -150,8 +160,6 @@
     ]
     for copy in inputs:
         copy.start()
-    lax.fori_loop(1, R, greet_row, 0)
-    lax.fori_loop(1, C, greet_col, 0)
 
     rows_p = lax.broadcasted_iota(jnp.int32, (PB, 128), 0)
     lane = lax.broadcasted_iota(jnp.int32, (1, 128), 1)
@@ -214,7 +222,7 @@
     tblk[r] = own
     town[k, z] = own
 
-    pl.semaphore_wait(barrier, C - 1 + R - 1)
+    pl.semaphore_wait(barrier, len(neighbours))
 
     mine = pl.ds(pl.multiple_of(color * SL, SL), SL)
     mine_a = pl.ds(pl.multiple_of(color * SL, HALF), HALF)
@@ -227,12 +235,20 @@
         a, b = (mine_a, mine_b) if last else (mine, mine)
         send(qbuf.at[up, a], qbuf.at[up, a], z_send.at[0, s - 1], z_recv.at[0, s - 1], row=row_of(z + 1, k))
         send(qbuf.at[down, b], qbuf.at[down, b], z_send.at[1, s - 1], z_recv.at[1, s - 1], row=row_of(z - 1, k))
+        table = spt.at[k, lax.div(up, 2)]
+        send(table, table, s_send.at[0, s - 1], s_recv.at[0, s - 1], row=row_of(z + 1, k))
+        if not last:
+            table = spt.at[k, lax.div(down, 2)]
+            send(table, table, s_send.at[1, s - 1], s_recv.at[1, s - 1], row=row_of(z - 1, k))
 
     def z_got(s):
         last = s == Z // 2
         a, b = (mine_a, mine_b) if last else (mine, mine)
         got(qbuf.at[row_of(z - s, k), a], z_recv.at[0, s - 1])
         got(qbuf.at[row_of(z + s, k), b], z_recv.at[1, s - 1])
+        got(spt.at[k, lax.div(row_of(z - s, k), 2)], s_recv.at[0, s - 1])
+        if not last:
+            got(spt.at[k, lax.div(row_of(z + s, k), 2)], s_recv.at[1, s - 1])
 
     offsets = []
     for s in range(1, Z // 2):
@@ -270,6 +286,38 @@
         got(qbuf.at[b], sib_recv.at[j])
         return b
 
+    def x_first():
+        for n, peer in enumerate((col_of(x + 1, y), col_of(x - 1, y))):
+            send(sqx.at[c], sqx.at[c], x_send.at[n], x_recv.at[n], col=peer)
+
+    def x_second():
+        back = col_of(x - 1, y)
+        got(sqx.at[back], x_recv.at[0])
+        send(sqx.at[back], sqx.at[back], x_send.at[2], x_recv.at[2], col=col_of(x + 1, y))
+
+    def x_last():
+        got(sqx.at[col_of(x + 1, y)], x_recv.at[1])
+        got(sqx.at[col_of(x - 2, y)], x_recv.at[2])
+
+    def chips(yy):
+        return sqx.at[pl.ds(col_of(0, yy), XC)]
+
+    def y_step(s):
+        up, down = chips(y - (s - 1)), chips(y + (s - 1))
+        send(up, up, y_send.at[0, s - 1], y_recv.at[0, s - 1], col=col_of(x, y + 1))
+        if s < YC // 2:
+            send(down, down, y_send.at[1, s - 1], y_recv.at[1, s - 1], col=col_of(x, y - 1))
+
+    def y_turn(s):
+        got(chips(y - s), y_recv.at[0, s - 1])
+        if s < YC // 2:
+            got(chips(y + s), y_recv.at[1, s - 1])
+            y_step(s + 1)
+
+    def x_last_and_y():
+        x_last()
+        y_step(1)
+
     def to_col(src_of, dst, n):
         def body(i, carry):
             peer = lax.rem(c + i, C)
@@ -299,11 +347,9 @@
 
     z_step(1)
     sib_step(0)
-    to_col(lambda peer: sqx.at[c], sqx.at[c], 0)
-    to_z(spt, 1)
+    x_first()
 
     def student_logits():
-        got(sqx.at[pl.ds(0, C - 1)], many_recv.at[0])
         got(spt.at[1 - k], many_recv.at[2])
         part = jnp.zeros((PB, 128), F32)
         order = [PR * (2 * zz + kk) + u for kk in range(2) for zz in range(Z) for u in range(PR)]
@@ -365,7 +411,6 @@
         zz_ = 2.0 * (jnp.exp(sbuf[...] - top) / mass) - jnp.where(onehot(), 1.0, 0.0)
         pack(upz, zz_, jnp.zeros((8, 128), F32))
         vbuf[c] = upz[c]
-        to_col(lambda peer: upz.at[peer], vbuf.at[c], 5)
         quarter = PB // GROUPS
         small = jnp.zeros((quarter, 128), F32)
         for g in range(GROUPS):
@@ -429,34 +474,54 @@
         for j in numbers(s):
             sib_got(j + 1)
 
+    student = [x_second, x_last_and_y, *[functools.partial(y_turn, t) for t in range(1, YC // 2 + 1)]]
+
+    def relay():
+        if student:
+            student.pop(0)()
+
+    def spt_to_sib():
+        send(spt.at[k], spt.at[k], many_send.at[2], many_recv.at[2], row=row_of(z, 1 - k))
+
+    def logits():
+        while student:
+            relay()
+        student_logits()
+        student_stats()
+
     teach([sib_got(0)])
     z_turn(1)
-    z_to_sib(spt, 1)
+    relay()
     if half >= 2:
         z_turn(2)
+        relay()
     whole(1)
     if half >= 2:
         teach(at(1, k))
+        relay()
         if half >= 3:
             z_turn(3)
-        student_logits()
-        student_stats()
         for s in range(2, half + 1):
             whole(s)
             if s + 2 <= half:
                 z_turn(s + 2)
+            if s + 2 == max(half, 4):
+                spt_to_sib()
             if s < half:
                 teach(at(s, k))
+                relay()
                 handed(s)
                 teach(at(s, 1 - k))
+                relay()
             else:
+                logits()
                 handed(s)
                 teach(at(s, k) + at(s, 1 - k))
         handed(1)
         teach(at(1, 1 - k))
     else:
-        student_logits()
-        student_stats()
+        spt_to_sib()
+        logits()
         handed(1)
         teach(at(1, k) + at(1, 1 - k))
 
@@ -477,11 +542,9 @@
     pack(upt, e, jnp.where(row8 == 0, top, jnp.where(row8 == 1, mass, cross)))
     ubuf[c] = upt[c]
     to_col(lambda peer: upt.at[peer], ubuf.at[c], 10)
+    to_col(lambda peer: upz.at[peer], vbuf.at[c], 5)
     z_to_sib(zag, 6)
     sq_tiles = unpack_queries()
-    got(vbuf.at[pl.ds(0, C - 1)], many_recv.at[5])
-    v_sum = functools.reduce(jnp.add, [vbuf[i] for i in range(C)])
-
     got(ubuf.at[pl.ds(0, C - 1)], many_recv.at[10])
     tops = only(jnp.concatenate([ubuf[i, 0:1] for i in range(C)], axis=0), 3)
     top = jnp.max(tops, axis=0, keepdims=True)
@@ -492,14 +555,16 @@
     whole = only(acc, 3)
     mass, cross = whole[1:2], whole[2:3]
     inverse = 1.0 / mass
-    grads = (SCALE / total) * (v_sum - acc * inverse)
-    for g in range(3):
-        qg_ref[8 * g : 8 * g + 8, :] = (pltpu.roll(grads, 128 - QB * g, 1) if g else grads)[:, 0:QB]
     per_query = cross * inverse - (top + jnp.log(mass)) + 2.0 * student_lse - hit
     fin[r] = jnp.where(lane_group == 0, top, jnp.where(lane_group == 1, inverse, per_query))
     to_row(lambda peer: fin.at[r], fin.at[r], 11)
     z_to_sib(tag, 8)
     unpack_slopes()
+    got(vbuf.at[pl.ds(0, C - 1)], many_recv.at[5])
+    v_sum = functools.reduce(jnp.add, [vbuf[i] for i in range(C)])
+    grads = (SCALE / total) * (v_sum - acc * inverse)
+    for g in range(3):
+        qg_ref[8 * g : 8 * g + 8, :] = (pltpu.roll(grads, 128 - QB * g, 1) if g else grads)[:, 0:QB]
     got(tag.at[1 - k], many_recv.at[9])
 
     got(fin.at[pl.ds(0, R - 1)], many_recv.at[11])
@@ -533,9 +598,20 @@
             left(qbuf.at[b, part], xy_send.at[n, j])
     for j in range(len(offsets) + 1):
         left(qbuf.at[r], sib_send.at[j])
-    for n, buf, count in ((0, sqx, C), (3, sst, C), (5, upz, C), (10, upt, C), (4, sqr, R), (11, fin, R), (12, tblk, R)):
+    for s in range(1, Z // 2 + 1):
+        left(spt.at[k, z], s_send.at[0, s - 1])
+        if s < Z // 2:
+            left(spt.at[k, z], s_send.at[1, s - 1])
+    for n in range(3):
+        left(sqx.at[c], x_send.at[n])
+    for s in range(1, YC // 2 + 1):
+        left(chips(y), y_send.at[0, s - 1])
+        if s < YC // 2:
+            left(chips(y), y_send.at[1, s - 1])
+    left(spt.at[k], many_send.at[2])
+    for n, buf, count in ((3, sst, C), (5, upz, C), (10, upt, C), (4, sqr, R), (11, fin, R), (12, tblk, R)):
         left(buf.at[pl.ds(0, count - 1)], many_send.at[n])
-    for n, buf in ((1, spt), (6, zag), (8, tag)):
+    for n, buf in ((6, zag), (8, tag)):
         left(buf.at[0, pl.ds(0, Z - 1)], many_send.at[n])
         left(buf.at[0], many_send.at[n + 1])
 
@@ -551,6 +627,7 @@
     DR = student_passages.shape[1]
     T = R // GROUPS
     hops = Z - 1
+    YC = C // min(X_CHIPS, C)
     dma = pltpu.SemaphoreType.DMA
     vmem = pl.BlockSpec(memory_space=pltpu.VMEM)
     hbm = pl.BlockSpec(memory_space=pltpu.HBM)
@@ -591,6 +668,12 @@
             dma((7,)),
             dma((2, Z // 2)),
             dma((2, Z // 2)),
+            dma((2, Z // 2)),
+            dma((2, Z // 2)),
+            dma((3,)),
+            dma((3,)),
+            dma((2, YC // 2)),
+            dma((2, YC // 2)),
             dma((4, hops)),
             dma((4, hops)),
             dma((hops + 1,)),

time: 68.6 us -> 69.3 us (1.010)
  Pallas kernels: 64 us -> 64.8 us
    pallas_call x1, Pallas kernels: 64 us -> 64.8 us  [shards(): pl.pallas_call(functools.partial(kernel, R, C), out_shape=(jax.ShapeDtype...]
where the time goes in v3:
time: 69.3 us; the launch traced here: 69.1 us
  Pallas kernels  64.8 us (94%)
  between operations  2.4 us (3%)
  local copies, waits for them, and re-layouts  1.92 us (3%)
    pallas_call x1, Pallas kernels, shards(): pl.pallas_call(functools.partial(kernel, R, C), out_shape=(jax.ShapeDtype...  64.8 us
    unnamed x4, local copies, waits for them, and re-layouts  1.92 us

profile of v3, /device:TPU:1, one launch (start us, length us, event | category | flops | bytes accessed | tf_op | source)
XLA Modules:
  0.0 69.1 jit_solution(17626298587472711648)
XLA Ops:
  0.6 64.8 %distill.1 = (f32[48,128]{1,0:T(8,128)}, f32[24,32]{1,0:T(8,128)}, f32[1,1]{1,0:T(1,128)}) custom-call(bf16[32,32,128]{2,1,0:T(8,128)(2,1)} %qt_hbm.1, s32[32]{0:T(128)} %qlen_hbm.1, bf16[8,176,128]{2,1,0:T(8,128)(2,1)} %pt_hbm.1, s32[8]{0:T(128)} %plen_hbm.1, bf16[24,32]{1,0:T(8,128)(2,1)} %bitcast.8, bf16[48,128]{1,0:T(8,128)(2,1)} %bitcast.7, s32[32]{0:T(128)} %pos_hbm.1), custom_call_target="tpu_custom_call" | custom-call | tf_op jit(solution)/shard_map/distill/pallas_call | solution.py:634
  65.4 0.0 copy-start
  65.5 1.3 %copy.13 = f32[32,24]{0,1:T(8,128)} copy(f32[32,24]{0,1:T(8,128)} %bitcast.6) | data formatting | bytes 6144
  66.8 0.0 copy-done
  66.8 0.6 copy.14
Async XLA Ops:
  65.4 1.3 %copy-start = (f32[48,128]{1,0:T(8,128)S(1)}, f32[48,128]{1,0:T(8,128)}, u32[]{:S(2)}) copy-start(f32[48,128]{1,0:T(8,128)} %get-tuple-element.7) | copy-start | bytes 73732

commit v4 on v2

--- a/solution.py
+++ b/solution.py
@@ -70,8 +70,12 @@
     tag,
     upt,
     ubuf,
+    tst,
+    sfin,
     fin,
     in_sem,
+    near_sem,
+    far_sem,
     z_send,
     z_recv,
     xy_send,
@@ -101,7 +105,7 @@
     k = lax.rem(r, 2)
     x = lax.rem(c, XC)
     y = lax.div(c, XC)
-    color = lax.rem(x + 2 * y, 4)
+    color = lax.rem(jnp.where(k == 0, x + 2 * y, 2 * x + y), 4)
 
     def row_of(zz, kk):
         return lax.rem(zz + 2 * Z, Z) * 2 + kk
@@ -126,13 +130,47 @@
 
     barrier = pltpu.get_barrier_semaphore()
 
-    def greet_col(i, carry):
-        pl.semaphore_signal(barrier, inc=1, device_id={"col": lax.rem(c + i, C)}, device_id_type=MESH)
-        return carry
-
-    def greet_row(i, carry):
-        pl.semaphore_signal(barrier, inc=1, device_id={"row": lax.rem(r + i, R)}, device_id_type=MESH)
-        return carry
+    def row_rank(rr):
+        return lax.div(rr, 2) * 2 + 1 - lax.rem(rr, 2)
+
+    def col_rank(cc):
+        yy = lax.div(cc, XC)
+        return jnp.where(yy < YC // 2, yy, YC // 2 + YC - 1 - yy) * XC + lax.rem(cc, XC)
+
+    row_place, col_place = row_rank(r), col_rank(c)
+    edges = (
+        ({"row": row_of(z, 1 - k)}, row_rank(row_of(z, 1 - k)) > row_place, 0),
+        ({"row": row_of(z + 1, k)}, row_rank(row_of(z + 1, k)) > row_place, 2),
+        ({"row": row_of(z - 1, k)}, row_rank(row_of(z - 1, k)) > row_place, 1),
+        ({"col": col_of(x + 1, y)}, col_rank(col_of(x + 1, y)) > col_place, 4),
+        ({"col": col_of(x - 1, y)}, col_rank(col_of(x - 1, y)) > col_place, 3),
+        ({"col": col_of(x, y + 1)}, col_rank(col_of(x, y + 1)) > col_place, 6),
+        ({"col": col_of(x, y - 1)}, col_rank(col_of(x, y - 1)) > col_place, 5),
+    )
+
+    def row_at(place):
+        return lax.div(place, 2) * 2 + 1 - lax.rem(place, 2)
+
+    def col_at(place):
+        yy = lax.div(place, XC)
+        return jnp.where(yy < YC // 2, yy, YC // 2 + YC - 1 - yy) * XC + lax.rem(place, XC)
+
+    def greet(sem, row_places, col_places):
+        def rows(i, carry):
+            pl.semaphore_signal(sem, inc=1, device_id={"row": row_at(i)}, device_id_type=MESH)
+            return carry
+
+        def cols(i, carry):
+            pl.semaphore_signal(sem, inc=1, device_id={"col": col_at(i)}, device_id_type=MESH)
+            return carry
+
+        lax.fori_loop(*row_places, rows, 0)
+        lax.fori_loop(*col_places, cols, 0)
+
+    def edge(n):
+        @pl.when(edges[n][1])
+        def _():
+            pl.semaphore_wait(near_sem.at[n], 1)
 
     inputs = [
         pltpu.make_async_copy(src, dst, in_sem.at[n])
@@ -150,8 +188,7 @@
     ]
     for copy in inputs:
         copy.start()
-    lax.fori_loop(1, R, greet_row, 0)
-    lax.fori_loop(1, C, greet_col, 0)
+    greet(barrier, (row_place + 1, R), (col_place + 1, C))
 
     rows_p = lax.broadcasted_iota(jnp.int32, (PB, 128), 0)
     lane = lax.broadcasted_iota(jnp.int32, (1, 128), 1)
@@ -168,6 +205,7 @@
         [jnp.where(slot < qlen_ref[i], qraw[i].astype(F32), 0.0) for i in range(QB)], axis=0
     )
     qbuf[r] = jnp.swapaxes(q32, 0, 1).reshape(N, 128).astype(BF)
+
 
     inputs[4].wait()
     inputs[5].wait()
@@ -214,30 +252,39 @@
     tblk[r] = own
     town[k, z] = own
 
-    pl.semaphore_wait(barrier, C - 1 + R - 1)
+    @pl.when(row_place + col_place > 0)
+    def _():
+        pl.semaphore_wait(barrier, row_place + col_place)
+
+    for peer, later, back in edges:
+
+        @pl.when(jnp.logical_not(later))
+        def _(peer=peer, back=back):
+            pl.semaphore_signal(near_sem.at[back], inc=1, device_id=peer, device_id_type=MESH)
+
 
     mine = pl.ds(pl.multiple_of(color * SL, SL), SL)
     mine_a = pl.ds(pl.multiple_of(color * SL, HALF), HALF)
     mine_b = pl.ds(pl.multiple_of(color * SL + HALF, HALF), HALF)
 
-    def z_step(s):
-        up = row_of(z - (s - 1), k)
-        down = row_of(z + (s - 1), k)
-        last = s == Z // 2
-        a, b = (mine_a, mine_b) if last else (mine, mine)
-        send(qbuf.at[up, a], qbuf.at[up, a], z_send.at[0, s - 1], z_recv.at[0, s - 1], row=row_of(z + 1, k))
-        send(qbuf.at[down, b], qbuf.at[down, b], z_send.at[1, s - 1], z_recv.at[1, s - 1], row=row_of(z - 1, k))
-
-    def z_got(s):
-        last = s == Z // 2
-        a, b = (mine_a, mine_b) if last else (mine, mine)
-        got(qbuf.at[row_of(z - s, k), a], z_recv.at[0, s - 1])
-        got(qbuf.at[row_of(z + s, k), b], z_recv.at[1, s - 1])
-
-    offsets = []
-    for s in range(1, Z // 2):
-        offsets += [s, -s]
-    offsets.append(Z // 2)
+    half = Z // 2
+    ways = (jnp.where(z < 2, 1, 0), jnp.where(z < 2, 0, 1))
+    levels = [[(w, s) for w in ways] for s in range(1, half)] + [[(0, half)]]
+    numbers = [[2 * n + w for w in range(len(level))] for n, level in enumerate(levels)]
+
+    def block(way, s, kk):
+        return row_of(z + (2 * way - 1) * s, kk)
+
+    blocks = [(way, s) for level in levels for way, s in level]
+
+    def z_step(way, s):
+        b = block(way, s - 1, k)
+        send(
+            qbuf.at[b, mine], qbuf.at[b, mine], z_send.at[way, s - 1], z_recv.at[way, s - 1], row=row_of(z + 1 - 2 * way, k)
+        )
+
+    def z_got(way, s):
+        got(qbuf.at[block(way, s, k), mine], z_recv.at[way, s - 1])
 
     def xy_regions():
         one = lax.rem(color + 3, 4) * SL
@@ -251,22 +298,24 @@
         )
 
     def xy_step(j):
-        b = row_of(z + offsets[j], k)
-        to = (col_of(x + 1, y), col_of(x - 1, y), col_of(x, y + 1), col_of(x, y - 1))
+        b = block(*blocks[j], k)
+        beside = (col_of(x + 1, y), col_of(x - 1, y))
+        above = (col_of(x, y + 1), col_of(x, y - 1))
+        to = [jnp.where(k == 0, a, b) for a, b in zip(beside + above, above + beside)]
         for n, (part, peer) in enumerate(zip((mine, mine, mine_a, mine_b), to)):
             send(qbuf.at[b, part], qbuf.at[b, part], xy_send.at[n, j], xy_recv.at[n, j], col=peer)
 
     def xy_got(j):
-        b = row_of(z + offsets[j], k)
+        b = block(*blocks[j], k)
         for n, part in enumerate(xy_regions()):
             got(qbuf.at[b, part], xy_recv.at[n, j])
 
     def sib_step(j):
-        b = r if j == 0 else row_of(z + offsets[j - 1], k)
+        b = r if j == 0 else block(*blocks[j - 1], k)
         send(qbuf.at[b], qbuf.at[b], sib_send.at[j], sib_recv.at[j], row=row_of(z, 1 - k))
 
     def sib_got(j):
-        b = row_of(z, 1 - k) if j == 0 else row_of(z + offsets[j - 1], 1 - k)
+        b = row_of(z, 1 - k) if j == 0 else block(*blocks[j - 1], 1 - k)
         got(qbuf.at[b], sib_recv.at[j])
         return b
 
@@ -293,18 +342,25 @@
 
         lax.fori_loop(1, Z, body, 0)
 
-    def z_to_sib(buf, n):
+    def z_to_sib(buf, n, m):
         got(buf.at[0, pl.ds(0, Z - 1)], many_recv.at[n])
-        send(buf.at[k], buf.at[k], many_send.at[n + 1], many_recv.at[n + 1], row=row_of(z, 1 - k))
-
-    z_step(1)
+        send(buf.at[k], buf.at[k], many_send.at[m], many_recv.at[m], row=row_of(z, 1 - k))
+
+    edge(0)
     sib_step(0)
-    to_col(lambda peer: sqx.at[c], sqx.at[c], 0)
-    to_z(spt, 1)
+    lead = jnp.where(z == 0, 0, 1)
+    for way in (lead, 1 - lead):
+
+        @pl.when(jnp.where(way == 0, edges[1][1], edges[2][1]))
+        def _(way=way):
+            pl.semaphore_wait(near_sem.at[1 + way], 1)
+
+        z_step(way, 1)
+    greet(far_sem, (0, row_place), (0, col_place))
 
     def student_logits():
         got(sqx.at[pl.ds(0, C - 1)], many_recv.at[0])
-        got(spt.at[1 - k], many_recv.at[2])
+        got(spt.at[1 - k], many_recv.at[14])
         part = jnp.zeros((PB, 128), F32)
         order = [PR * (2 * zz + kk) + u for kk in range(2) for zz in range(Z) for u in range(PR)]
         rhs = jnp.concatenate([sqx[i] for i in order], axis=0).astype(BF)
@@ -313,7 +369,14 @@
             wide = spt[:, :, 8 * PR * g : 8 * PR * (g + 1), :].reshape(2 * Z * 8 * PR, PB)
             back = nt(unit, wide).astype(BF)
             part = jnp.where(lane_group == g, nn(back, rhs), part)
-        sbuf[...] = SCALE * spread(part)
+        s = SCALE * spread(part)
+        sbuf[...] = s
+        quarter = PB // GROUPS
+        small = jnp.zeros((quarter, 128), F32)
+        for g in range(GROUPS):
+            small = jnp.where(lane_group == g, s[quarter * g : quarter * (g + 1)], small)
+        zag[k, z] = small
+        to_z(zag, 6)
 
     p_index = c * PB + natural(rows_p)
 
@@ -337,7 +400,7 @@
     def only(v, g):
         return spread(jnp.where(lane_group == g, v, 0.0))
 
-    def pack(dst, weights, stats):
+    def pack(dst, weights):
         hi, lo = split2(weights)
         table = spt[...].reshape(2 * Z * DR, PB)
         u = nn(jnp.concatenate([table, table], axis=1), jnp.concatenate([hi, lo], axis=0))
@@ -345,38 +408,47 @@
             for zz in range(Z):
                 for uu in range(PR):
                     base = (kk * Z + zz) * DR + 8 * uu
-                    piece = stats
+                    piece = jnp.zeros((8, 128), F32)
                     for g in range(3):
                         at = base + 8 * PR * g
                         piece = jnp.where(lane_group == g, u[at : at + 8], piece)
                     dst[PR * (2 * zz + kk) + uu] = piece
 
+    def softmax_parts(buf):
+        rows = jnp.concatenate([buf[i] for i in range(C)], axis=0)
+        tops = only(rows, 0)
+        top = jnp.max(tops, axis=0, keepdims=True)
+        weights = jnp.exp(tops - top)
+        mass = only(jnp.sum(jnp.where(lane_group == 1, weights * rows, 0.0), axis=0, keepdims=True), 1)
+        return top, mass, only(jnp.sum(rows, axis=0, keepdims=True), 2), weights
+
     def student_slopes():
         got(sst.at[pl.ds(0, C - 1)], many_recv.at[3])
-        rows = [sst[i] for i in range(C)]
-        top = only(functools.reduce(jnp.maximum, rows), 0)
-        mass = jnp.zeros((1, 128), F32)
-        hit = jnp.zeros((1, 128), F32)
-        for v in rows:
-            mass = mass + jnp.where(lane_group == 0, jnp.exp(jnp.minimum(v - top, 0.0)) * pltpu.roll(v, 96, 1), 0.0)
-            hit = hit + v
-        mass = spread(mass)
-        hit = only(hit, 2)
+        top, mass, hit, _ = softmax_parts(sst)
         zz_ = 2.0 * (jnp.exp(sbuf[...] - top) / mass) - jnp.where(onehot(), 1.0, 0.0)
-        pack(upz, zz_, jnp.zeros((8, 128), F32))
+        pack(upz, zz_)
         vbuf[c] = upz[c]
         to_col(lambda peer: upz.at[peer], vbuf.at[c], 5)
-        quarter = PB // GROUPS
-        small = jnp.zeros((quarter, 128), F32)
-        for g in range(GROUPS):
-            small = jnp.where(lane_group == g, zz_[quarter * g : quarter * (g + 1)], small)
-        zag[k, z] = small
-        to_z(zag, 6)
+        wanted = jnp.zeros((1, 128), F32)
+        within = lax.rem(lane, QB)
+        for i in range(QB):
+            wanted = jnp.where(within == i, pos_ref[i].astype(F32), wanted)
+        sfin[r] = jnp.where(lane_group == 0, top, jnp.where(lane_group == 1, 1.0 / mass, wanted))
+        to_row(lambda peer: sfin.at[r], sfin.at[r], 2)
         return top + jnp.log(mass), hit
+
+    def row_vector(buf, t, g):
+        tile = jnp.zeros((1, 128), F32)
+        for b in range(GROUPS):
+            v = buf[GROUPS * t + b]
+            tile = jnp.where(lane_group == b, pltpu.roll(v, ((b - g) % GROUPS) * QB, 1) if b != g else v, tile)
+        return tile
 
     def unpack_slopes():
         got(zag.at[1 - k], many_recv.at[7])
+        got(sfin.at[pl.ds(0, R - 1)], many_recv.at[2])
         quarter = PB // GROUPS
+        places = p_index.astype(F32)
         for t in range(T):
             for g in range(GROUPS):
                 tile = jnp.zeros((quarter, 128), F32)
@@ -387,6 +459,8 @@
                         v = pltpu.roll(v, ((b - g) % GROUPS) * QB, 1)
                     tile = jnp.where(lane_group == b, v, tile)
                 zfull[t, quarter * g : quarter * (g + 1)] = tile
+            probs = jnp.exp(zfull[t] - row_vector(sfin, t, 0)) * row_vector(sfin, t, 1)
+            zfull[t] = 2.0 * probs - jnp.where(places == row_vector(sfin, t, 2), 1.0, 0.0)
 
     def unpack_queries():
         got(sqr.at[pl.ds(0, R - 1)], many_recv.at[4])
@@ -405,114 +479,111 @@
             tiles.append(jnp.concatenate(rows, axis=0).astype(BF))
         return tiles
 
-    half = Z // 2
-
-    def at(s, kk):
-        return [row_of(z + o, kk) for o in offsets if abs(o) == s]
-
-    def numbers(s):
-        return [j for j, o in enumerate(offsets) if abs(o) == s]
-
-    def z_turn(s):
-        z_got(s)
-        if s < half:
-            z_step(s + 1)
-        for j in numbers(s):
-            xy_step(j)
-
-    def whole(s):
-        for j in numbers(s):
-            xy_got(j)
-            sib_step(j + 1)
-
-    def handed(s):
-        for j in numbers(s):
-            sib_got(j + 1)
-
+    def turn(n):
+        for (way, s), number in zip(levels[n], numbers[n]):
+            z_got(way, s)
+            if s < half - 1:
+                z_step(way, s + 1)
+            if n == 0 and number == 0:
+                for e in (3, 4, 5, 6):
+                    edge(e)
+            xy_step(number)
+        if n == half - 2:
+            z_step(0, half)
+
+    def whole(n):
+        for number in numbers[n]:
+            xy_got(number)
+            sib_step(number + 1)
+
+    def handed(n):
+        for number in numbers[n]:
+            sib_got(number + 1)
+
+    def at(n, kk):
+        return [block(way, s, kk) for way, s in levels[n]]
+
+    turn(0)
     teach([sib_got(0)])
-    z_turn(1)
-    z_to_sib(spt, 1)
-    if half >= 2:
-        z_turn(2)
-    whole(1)
-    if half >= 2:
-        teach(at(1, k))
-        if half >= 3:
-            z_turn(3)
-        student_logits()
-        student_stats()
-        for s in range(2, half + 1):
-            whole(s)
-            if s + 2 <= half:
-                z_turn(s + 2)
-            if s < half:
-                teach(at(s, k))
-                handed(s)
-                teach(at(s, 1 - k))
-            else:
-                handed(s)
-                teach(at(s, k) + at(s, 1 - k))
-        handed(1)
-        teach(at(1, 1 - k))
-    else:
-        student_logits()
-        student_stats()
-        handed(1)
-        teach(at(1, k) + at(1, 1 - k))
+    turn(1)
+    whole(0)
+
+    @pl.when(row_place + col_place < R + C - 2)
+    def _():
+        pl.semaphore_wait(far_sem, R - 1 - row_place + C - 1 - col_place)
+
+    to_col(lambda peer: sqx.at[c], sqx.at[c], 0)
+    to_z(spt, 1)
+    teach(at(0, k))
+    for n in range(1, half):
+        if n + 1 < half:
+            turn(n + 1)
+        if n == half - 1:
+            student_logits()
+            student_stats()
+        whole(n)
+        if n < half - 1:
+            teach(at(n, k))
+            handed(n)
+            teach(at(n, 1 - k))
+        if n == max(half - 3, 1):
+            z_to_sib(spt, 1, 14)
+        if n == half - 1:
+            handed(n)
+            teach(at(n, k) + at(n, 1 - k))
+    handed(0)
+    teach(at(0, 1 - k))
 
     for t in range(T):
         tile = tblk[GROUPS * t]
         for b in range(1, GROUPS):
             tile = jnp.where(lane_group == b, tblk[GROUPS * t + b], tile)
         tag[k, z, t] = tile
-    to_z(tag, 8)
     student_lse, hit = student_slopes()
+    z_to_sib(zag, 6, 7)
     got(tblk.at[pl.ds(0, R - 1)], many_recv.at[12])
     t_own = town[...].reshape(PB, 128)
     top = jnp.max(t_own, axis=0, keepdims=True)
     e = jnp.exp(t_own - top)
     mass = jnp.sum(e, axis=0, keepdims=True)
     cross = jnp.sum(e * (t_own - sbuf[...]), axis=0, keepdims=True)
-    row8 = lax.broadcasted_iota(jnp.int32, (8, 128), 0)
-    pack(upt, e, jnp.where(row8 == 0, top, jnp.where(row8 == 1, mass, cross)))
+    tst[c] = jnp.where(lane_group == 0, top, jnp.where(lane_group == 1, mass, cross))
+    to_col(lambda peer: tst.at[c], tst.at[c], 13)
+    pack(upt, e)
     ubuf[c] = upt[c]
     to_col(lambda peer: upt.at[peer], ubuf.at[c], 10)
-    z_to_sib(zag, 6)
+    to_z(tag, 8)
     sq_tiles = unpack_queries()
     got(vbuf.at[pl.ds(0, C - 1)], many_recv.at[5])
     v_sum = functools.reduce(jnp.add, [vbuf[i] for i in range(C)])
-
+    unpack_slopes()
+
+    got(tst.at[pl.ds(0, C - 1)], many_recv.at[13])
+    top, mass, _, weights = softmax_parts(tst)
+    rows = jnp.concatenate([tst[i] for i in range(C)], axis=0)
+    cross = only(jnp.sum(weights * rows, axis=0, keepdims=True), 2)
+    inverse = 1.0 / mass
+    per_query = cross * inverse - (top + jnp.log(mass)) + 2.0 * student_lse - hit
+    fin[r] = jnp.where(lane_group == 0, top, jnp.where(lane_group == 1, inverse, per_query))
+    to_row(lambda peer: fin.at[r], fin.at[r], 11)
+    z_to_sib(tag, 8, 9)
     got(ubuf.at[pl.ds(0, C - 1)], many_recv.at[10])
-    tops = only(jnp.concatenate([ubuf[i, 0:1] for i in range(C)], axis=0), 3)
-    top = jnp.max(tops, axis=0, keepdims=True)
-    weights = jnp.exp(tops - top)
     acc = jnp.zeros((8, 128), F32)
     for i in range(C):
         acc = acc + weights[i : i + 1] * ubuf[i]
-    whole = only(acc, 3)
-    mass, cross = whole[1:2], whole[2:3]
-    inverse = 1.0 / mass
     grads = (SCALE / total) * (v_sum - acc * inverse)
     for g in range(3):
         qg_ref[8 * g : 8 * g + 8, :] = (pltpu.roll(grads, 128 - QB * g, 1) if g else grads)[:, 0:QB]
-    per_query = cross * inverse - (top + jnp.log(mass)) + 2.0 * student_lse - hit
-    fin[r] = jnp.where(lane_group == 0, top, jnp.where(lane_group == 1, inverse, per_query))
-    to_row(lambda peer: fin.at[r], fin.at[r], 11)
-    z_to_sib(tag, 8)
-    unpack_slopes()
     got(tag.at[1 - k], many_recv.at[9])
 
     got(fin.at[pl.ds(0, R - 1)], many_recv.at[11])
     grads = jnp.zeros((DR, PB), F32)
     per_query = jnp.zeros((1, 128), F32)
     for t in range(T):
-        tops = jnp.zeros((1, 128), F32)
-        inverses = jnp.zeros((1, 128), F32)
+        tops = row_vector(fin, t, 0)
+        inverses = row_vector(fin, t, 1)
         for b in range(GROUPS):
-            v = fin[GROUPS * t + b]
-            per_query = per_query + jnp.where(lane_group == 2, v, 0.0)
-            tops = jnp.where(lane_group == b, pltpu.roll(v, b * QB, 1) if b else v, tops)
-            inverses = jnp.where(lane_group == b, pltpu.roll(v, ((b - 1) % GROUPS) * QB, 1) if b != 1 else v, inverses)
+            per_query = per_query + jnp.where(lane_group == 2, fin[GROUPS * t + b], 0.0)
         slopes = zfull[t] - jnp.exp(tag[:, :, t].reshape(PB, 128) - tops) * inverses
         slopes = jnp.concatenate(
             [slopes[8 * (kk * Z + zz) : 8 * (kk * Z + zz) + 8] for zz in range(Z) for kk in range(2)], axis=0
@@ -522,22 +593,20 @@
     pg_ref[...] = grads * (SCALE / total)
     loss_ref[...] = jnp.zeros((1, 1), F32) + jnp.sum(per_query) / total
 
-    for s in range(1, Z // 2 + 1):
-        last = s == Z // 2
-        a, b = (mine_a, mine_b) if last else (mine, mine)
-        left(qbuf.at[row_of(z - (s - 1), k), a], z_send.at[0, s - 1])
-        left(qbuf.at[row_of(z + (s - 1), k), b], z_send.at[1, s - 1])
-    for j in range(len(offsets)):
-        b = row_of(z + offsets[j], k)
+    for s in range(1, half + 1):
+        left(qbuf.at[r, mine], z_send.at[0, s - 1])
+        if s < half:
+            left(qbuf.at[r, mine], z_send.at[1, s - 1])
+    for j in range(len(blocks)):
         for n, part in enumerate((mine, mine, mine_a, mine_b)):
-            left(qbuf.at[b, part], xy_send.at[n, j])
-    for j in range(len(offsets) + 1):
+            left(qbuf.at[r, part], xy_send.at[n, j])
+    for j in range(len(blocks) + 1):
         left(qbuf.at[r], sib_send.at[j])
-    for n, buf, count in ((0, sqx, C), (3, sst, C), (5, upz, C), (10, upt, C), (4, sqr, R), (11, fin, R), (12, tblk, R)):
+    for n, buf, count in ((0, sqx, C), (2, sfin, R), (13, tst, C), (3, sst, C), (5, upz, C), (10, upt, C), (4, sqr, R), (11, fin, R), (12, tblk, R)):
         left(buf.at[pl.ds(0, count - 1)], many_send.at[n])
-    for n, buf in ((1, spt), (6, zag), (8, tag)):
+    for n, m, buf in ((1, 14, spt), (6, 7, zag), (8, 9, tag)):
         left(buf.at[0, pl.ds(0, Z - 1)], many_send.at[n])
-        left(buf.at[0], many_send.at[n + 1])
+        left(buf.at[0], many_send.at[m])
 
 
 def shards(query_tokens, query_lengths, passage_tokens, passage_lengths, student_queries, student_passages, positives):
@@ -587,16 +656,20 @@
             pltpu.VMEM((2, Z, T, 8, 128), F32),
             pltpu.VMEM((C, 8, 128), F32),
             pltpu.VMEM((C, 8, 128), F32),
+            pltpu.VMEM((C, 1, 128), F32),
+            pltpu.VMEM((R, 1, 128), F32),
             pltpu.VMEM((R, 1, 128), F32),
             dma((7,)),
+            pltpu.SemaphoreType.REGULAR((7,)),
+            pltpu.SemaphoreType.REGULAR,
             dma((2, Z // 2)),
             dma((2, Z // 2)),
             dma((4, hops)),
             dma((4, hops)),
             dma((hops + 1,)),
             dma((hops + 1,)),
-            dma((13,)),
-            dma((13,)),
+            dma((15,)),
+            dma((15,)),
         ],
         compiler_params=pltpu.CompilerParams(
             collective_id=0, has_side_effects=True, vmem_limit_bytes=64 * 1024 * 1024

time: 68.6 us -> 63.4 us (0.924)
  Pallas kernels: 64 us -> 58.8 us
    pallas_call x1, Pallas kernels: 64 us -> 58.8 us  [shards(): pl.pallas_call(functools.partial(kernel, R, C), out_shape=(jax.ShapeDtype...]
where the time goes in v4:
time: 63.4 us; the launch traced here: 63.2 us
  Pallas kernels  58.8 us (93%)
  between operations  2.4 us (4%)
  local copies, waits for them, and re-layouts  1.92 us (3%)
    pallas_call x1, Pallas kernels, shards(): pl.pallas_call(functools.partial(kernel, R, C), out_shape=(jax.ShapeDtype...  58.8 us
    unnamed x4, local copies, waits for them, and re-layouts  1.92 us

profile of v4, /device:TPU:1, one launch (start us, length us, event | category | flops | bytes accessed | tf_op | source)
XLA Modules:
  0.0 63.2 jit_solution(11425512342767143546)
XLA Ops:
  0.6 58.8 %distill.1 = (f32[48,128]{1,0:T(8,128)}, f32[24,32]{1,0:T(8,128)}, f32[1,1]{1,0:T(1,128)}) custom-call(bf16[32,32,128]{2,1,0:T(8,128)(2,1)} %qt_hbm.1, s32[32]{0:T(128)} %qlen_hbm.1, bf16[8,176,128]{2,1,0:T(8,128)(2,1)} %pt_hbm.1, s32[8]{0:T(128)} %plen_hbm.1, bf16[24,32]{1,0:T(8,128)(2,1)} %bitcast.8, bf16[48,128]{1,0:T(8,128)(2,1)} %bitcast.7, s32[32]{0:T(128)} %pos_hbm.1), custom_call_target="tpu_custom_call" | custom-call | tf_op jit(solution)/shard_map/distill/pallas_call | solution.py:626
  59.5 0.0 copy-start
  59.5 1.3 %copy.13 = f32[32,24]{0,1:T(8,128)} copy(f32[32,24]{0,1:T(8,128)} %bitcast.6) | data formatting | bytes 6144
  60.8 0.0 copy-done
  60.8 0.6 copy.14
Async XLA Ops:
  59.5 1.3 %copy-start = (f32[48,128]{1,0:T(8,128)S(1)}, f32[48,128]{1,0:T(8,128)}, u32[]{:S(2)}) copy-start(f32[48,128]{1,0:T(8,128)} %get-tuple-element.7) | copy-start | bytes 73732

commit v5 on v4

--- a/solution.py
+++ b/solution.py
@@ -50,6 +50,7 @@
     qlen_ref,
     plen_ref,
     pos_ref,
+    wanted_ref,
     sq_ref,
     sp_ref,
     qraw,
@@ -194,17 +195,13 @@
     lane = lax.broadcasted_iota(jnp.int32, (1, 128), 1)
     lane_group = lax.div(lane, QB)
 
-    def natural(i):
-        rank = lax.div(i, 8)
-        return (2 * lax.rem(rank, Z) + lax.div(rank, Z)) * 8 + lax.rem(i, 8)
-
     inputs[0].wait()
     inputs[1].wait()
     slot = lax.broadcasted_iota(jnp.int32, (L, 128), 0)
     q32 = jnp.stack(
         [jnp.where(slot < qlen_ref[i], qraw[i].astype(F32), 0.0) for i in range(QB)], axis=0
     )
-    qbuf[r] = jnp.swapaxes(q32, 0, 1).reshape(N, 128).astype(BF)
+    qbuf[z] = jnp.swapaxes(q32, 0, 1).reshape(N, 128).astype(BF)
 
 
     inputs[4].wait()
@@ -216,41 +213,40 @@
     for g in range(3):
         packed = jnp.where(lane_group == g, sq_wide[8 * g : 8 * g + 8], packed)
     sqx[c] = packed
-    pa = lax.broadcasted_iota(jnp.int32, (PB, PB), 0)
-    pb = lax.broadcasted_iota(jnp.int32, (PB, PB), 1)
-    sp_wide = nn(sp_ref[...], (pa == natural(pb)).astype(BF))
+    sp_wide = sp_ref[...].astype(F32)
     spt[k, z] = jnp.concatenate(
         [sp_wide[24 * u + 8 * g : 24 * u + 8 * g + 8] for g in range(3) for u in range(PR)], axis=0
     ).astype(BF)
 
+    inputs[6].wait()
+    wanted = jnp.zeros((1, 128), F32)
+    within = lax.rem(lane, QB)
+    for i in range(QB):
+        wanted = jnp.where(within == i, pos_ref[i].astype(F32), wanted)
+    wanted_ref[...] = wanted
+
     inputs[2].wait()
     inputs[3].wait()
-    inputs[6].wait()
     pslot = lax.broadcasted_iota(jnp.int32, (LP, 128), 0)
     p32 = []
     for i in range(8):
         rows = praw[i].astype(F32)
         p32.append(jnp.where(pslot < plen_ref[i], rows, rows[0:1]))
-    xbuf[...] = jnp.swapaxes(jnp.stack(p32, axis=0), 0, 1).reshape(LP * 8, 128).astype(BF)
-
-    def maxsim(b):
-        s = nt(xbuf[...], qbuf[b])
-        m = jnp.max(s.reshape(LP, 8, N), axis=0)
+    xbuf[k] = jnp.swapaxes(jnp.stack(p32, axis=0), 0, 1).reshape(LP * 8, 128).astype(BF)
+
+    def maxsim(tokens, zz):
+        s = nt(tokens, qbuf[zz])
+        m = jnp.max(s.reshape(-1, LP, 8, N), axis=1).reshape(-1, N)
         acc = m[:, 0:128]
         for t in range(1, N // 128):
             acc = acc + m[:, 128 * t : 128 * t + 128]
         return spread(acc)
 
-    def teach(blocks):
-        found = [maxsim(b) for b in blocks]
-        for b, v in zip(blocks, found):
-            tblk[b] = v
-        for b in blocks:
-            send(tblk.at[b], town.at[k, z], many_send.at[12], many_recv.at[12], row=b)
-
-    own = maxsim(r)
-    tblk[r] = own
-    town[k, z] = own
+    def teach(zz):
+        tblk[zz] = maxsim(xbuf[...].reshape(2 * LP * 8, 128), zz).reshape(2, 8, 128)
+        send(tblk.at[zz], town.at[z], many_send.at[12], many_recv.at[12], row=row_of(zz, k))
+
+    tblk[z, k] = maxsim(xbuf[k], z)
 
     @pl.when(row_place + col_place > 0)
     def _():
@@ -272,19 +268,19 @@
     levels = [[(w, s) for w in ways] for s in range(1, half)] + [[(0, half)]]
     numbers = [[2 * n + w for w in range(len(level))] for n, level in enumerate(levels)]
 
-    def block(way, s, kk):
-        return row_of(z + (2 * way - 1) * s, kk)
+    def block(way, s):
+        return lax.rem(z + (2 * way - 1) * s + Z, Z)
 
     blocks = [(way, s) for level in levels for way, s in level]
 
     def z_step(way, s):
-        b = block(way, s - 1, k)
+        b = block(way, s - 1)
         send(
             qbuf.at[b, mine], qbuf.at[b, mine], z_send.at[way, s - 1], z_recv.at[way, s - 1], row=row_of(z + 1 - 2 * way, k)
         )
 
     def z_got(way, s):
-        got(qbuf.at[block(way, s, k), mine], z_recv.at[way, s - 1])
+        got(qbuf.at[block(way, s), mine], z_recv.at[way, s - 1])
 
     def xy_regions():
         one = lax.rem(color + 3, 4) * SL
@@ -298,7 +294,7 @@
         )
 
     def xy_step(j):
-        b = block(*blocks[j], k)
+        b = block(*blocks[j])
         beside = (col_of(x + 1, y), col_of(x - 1, y))
         above = (col_of(x, y + 1), col_of(x, y - 1))
         to = [jnp.where(k == 0, a, b) for a, b in zip(beside + above, above + beside)]
@@ -306,22 +302,17 @@
             send(qbuf.at[b, part], qbuf.at[b, part], xy_send.at[n, j], xy_recv.at[n, j], col=peer)
 
     def xy_got(j):
-        b = block(*blocks[j], k)
+        b = block(*blocks[j])
         for n, part in enumerate(xy_regions()):
             got(qbuf.at[b, part], xy_recv.at[n, j])
 
-    def sib_step(j):
-        b = r if j == 0 else block(*blocks[j - 1], k)
-        send(qbuf.at[b], qbuf.at[b], sib_send.at[j], sib_recv.at[j], row=row_of(z, 1 - k))
-
-    def sib_got(j):
-        b = row_of(z, 1 - k) if j == 0 else block(*blocks[j - 1], 1 - k)
-        got(qbuf.at[b], sib_recv.at[j])
-        return b
+    def far_first(i, n):
+        step = lax.div(i, 2)
+        return n // 2 + jnp.where(lax.rem(i, 2) == 0, step, -step)
 
     def to_col(src_of, dst, n):
         def body(i, carry):
-            peer = lax.rem(c + i, C)
+            peer = lax.rem(c + far_first(i, C), C)
             send(src_of(peer), dst, many_send.at[n], many_recv.at[n], col=peer)
             return carry
 
@@ -329,7 +320,7 @@
 
     def to_row(src_of, dst, n):
         def body(i, carry):
-            peer = lax.rem(r + i, R)
+            peer = lax.rem(r + far_first(i, R), R)
             send(src_of(peer), dst, many_send.at[n], many_recv.at[n], row=peer)
             return carry
 
@@ -346,8 +337,6 @@
         got(buf.at[0, pl.ds(0, Z - 1)], many_recv.at[n])
         send(buf.at[k], buf.at[k], many_send.at[m], many_recv.at[m], row=row_of(z, 1 - k))
 
-    edge(0)
-    sib_step(0)
     lead = jnp.where(z == 0, 0, 1)
     for way in (lead, 1 - lead):
 
@@ -356,44 +345,44 @@
             pl.semaphore_wait(near_sem.at[1 + way], 1)
 
         z_step(way, 1)
+    edge(0)
+    send(xbuf.at[k], xbuf.at[k], sib_send, sib_recv, row=row_of(z, 1 - k))
     greet(far_sem, (0, row_place), (0, col_place))
 
-    def student_logits():
-        got(sqx.at[pl.ds(0, C - 1)], many_recv.at[0])
-        got(spt.at[1 - k], many_recv.at[14])
+    p_index = c * PB + rows_p
+
+    def onehot():
+        return p_index.astype(F32) == wanted_ref[...]
+
+    def student_scores():
         part = jnp.zeros((PB, 128), F32)
         order = [PR * (2 * zz + kk) + u for kk in range(2) for zz in range(Z) for u in range(PR)]
         rhs = jnp.concatenate([sqx[i] for i in order], axis=0).astype(BF)
-        unit = (pa == pb).astype(BF)
+        unit = lax.broadcasted_iota(jnp.int32, (PB, PB), 0) == lax.broadcasted_iota(jnp.int32, (PB, PB), 1)
+        unit = unit.astype(BF)
         for g in range(3):
             wide = spt[:, :, 8 * PR * g : 8 * PR * (g + 1), :].reshape(2 * Z * 8 * PR, PB)
             back = nt(unit, wide).astype(BF)
             part = jnp.where(lane_group == g, nn(back, rhs), part)
         s = SCALE * spread(part)
-        sbuf[...] = s
         quarter = PB // GROUPS
         small = jnp.zeros((quarter, 128), F32)
         for g in range(GROUPS):
             small = jnp.where(lane_group == g, s[quarter * g : quarter * (g + 1)], small)
-        zag[k, z] = small
-        to_z(zag, 6)
-
-    p_index = c * PB + natural(rows_p)
-
-    def onehot():
-        wanted = jnp.zeros((1, 128), jnp.int32)
-        within = lax.rem(lane, QB)
-        for i in range(QB):
-            wanted = jnp.where(within == i, pos_ref[i], wanted)
-        return p_index == wanted
-
-    def student_stats():
-        s = sbuf[...]
         top = jnp.max(s, axis=0, keepdims=True)
         mass = jnp.sum(jnp.exp(s - top), axis=0, keepdims=True)
         hit = jnp.sum(jnp.where(onehot(), s, 0.0), axis=0, keepdims=True)
-        sst[c] = jnp.where(lane_group == 0, top, jnp.where(lane_group == 1, mass, hit))
+        return s, small, jnp.where(lane_group == 0, top, jnp.where(lane_group == 1, mass, hit))
+
+    def score_student():
+        got(sqx.at[pl.ds(0, C - 1)], many_recv.at[0])
+        got(spt.at[1 - k], many_recv.at[14])
+        s, small, parts = student_scores()
+        sbuf[...] = s
+        zag[k, z] = small
+        sst[c] = parts
         to_col(lambda peer: sst.at[c], sst.at[c], 3)
+        to_z(zag, 6)
         to_row(lambda peer: sqx.at[pl.ds(PR * peer, PR)], sqr.at[r], 4)
         sqr[r] = sqx[pl.ds(PR * r, PR)]
 
@@ -429,18 +418,17 @@
         pack(upz, zz_)
         vbuf[c] = upz[c]
         to_col(lambda peer: upz.at[peer], vbuf.at[c], 5)
-        wanted = jnp.zeros((1, 128), F32)
-        within = lax.rem(lane, QB)
-        for i in range(QB):
-            wanted = jnp.where(within == i, pos_ref[i].astype(F32), wanted)
-        sfin[r] = jnp.where(lane_group == 0, top, jnp.where(lane_group == 1, 1.0 / mass, wanted))
+        sfin[r] = jnp.where(lane_group == 0, top, jnp.where(lane_group == 1, 1.0 / mass, wanted_ref[...]))
         to_row(lambda peer: sfin.at[r], sfin.at[r], 2)
         return top + jnp.log(mass), hit
+
+    def owner(t, b):
+        return 2 * (GROUPS * (t % (T // 2)) + b) + t // (T // 2)
 
     def row_vector(buf, t, g):
         tile = jnp.zeros((1, 128), F32)
         for b in range(GROUPS):
-            v = buf[GROUPS * t + b]
+            v = buf[owner(t, b)]
             tile = jnp.where(lane_group == b, pltpu.roll(v, ((b - g) % GROUPS) * QB, 1) if b != g else v, tile)
         return tile
 
@@ -453,7 +441,7 @@
             for g in range(GROUPS):
                 tile = jnp.zeros((quarter, 128), F32)
                 for b in range(GROUPS):
-                    rr = GROUPS * t + b
+                    rr = owner(t, b)
                     v = zag[rr % 2, rr // 2]
                     if b != g:
                         v = pltpu.roll(v, ((b - g) % GROUPS) * QB, 1)
@@ -471,7 +459,7 @@
                 for g in range(3):
                     tile = jnp.zeros((8, 128), F32)
                     for b in range(GROUPS):
-                        v = sqr[GROUPS * t + b, u]
+                        v = sqr[owner(t, b), u]
                         if b != g:
                             v = pltpu.roll(v, ((b - g) % GROUPS) * QB, 1)
                         tile = jnp.where(lane_group == b, v, tile)
@@ -479,34 +467,27 @@
             tiles.append(jnp.concatenate(rows, axis=0).astype(BF))
         return tiles
 
-    def turn(n):
-        for (way, s), number in zip(levels[n], numbers[n]):
-            z_got(way, s)
-            if s < half - 1:
-                z_step(way, s + 1)
-            if n == 0 and number == 0:
-                for e in (3, 4, 5, 6):
-                    edge(e)
-            xy_step(number)
+    def turn(n, w):
+        way, s = levels[n][w]
+        z_got(way, s)
+        if s < half - 1:
+            z_step(way, s + 1)
         if n == half - 2:
-            z_step(0, half)
-
-    def whole(n):
-        for number in numbers[n]:
-            xy_got(number)
-            sib_step(number + 1)
-
-    def handed(n):
-        for number in numbers[n]:
-            sib_got(number + 1)
-
-    def at(n, kk):
-        return [block(way, s, kk) for way, s in levels[n]]
-
-    turn(0)
-    teach([sib_got(0)])
-    turn(1)
-    whole(0)
+
+            @pl.when(way == 0)
+            def _():
+                z_step(0, half)
+
+        if n == 0 and w == 0:
+            for e in (3, 4, 5, 6):
+                edge(e)
+        xy_step(numbers[n][w])
+
+    turn(0, 0)
+    turn(0, 1)
+    got(xbuf.at[1 - k], sib_recv)
+    tblk[z, 1 - k] = maxsim(xbuf[1 - k], z)
+    town[z] = tblk[z]
 
     @pl.when(row_place + col_place < R + C - 2)
     def _():
@@ -514,34 +495,27 @@
 
     to_col(lambda peer: sqx.at[c], sqx.at[c], 0)
     to_z(spt, 1)
-    teach(at(0, k))
-    for n in range(1, half):
-        if n + 1 < half:
-            turn(n + 1)
-        if n == half - 1:
-            student_logits()
-            student_stats()
-        whole(n)
+    last = len(blocks) - 1
+    for j in range(len(blocks)):
+        n, w = j // 2 + 1, j % 2
         if n < half - 1:
-            teach(at(n, k))
-            handed(n)
-            teach(at(n, 1 - k))
-        if n == max(half - 3, 1):
+            turn(n, w)
+        if j == min(3, last - 1):
             z_to_sib(spt, 1, 14)
-        if n == half - 1:
-            handed(n)
-            teach(at(n, k) + at(n, 1 - k))
-    handed(0)
-    teach(at(0, 1 - k))
-
-    for t in range(T):
+        if j == min(4, last):
+            turn(half - 1, 0)
+            score_student()
+        xy_got(j)
+        teach(block(*blocks[j]))
+
+    for t in range(T // 2):
         tile = tblk[GROUPS * t]
         for b in range(1, GROUPS):
             tile = jnp.where(lane_group == b, tblk[GROUPS * t + b], tile)
         tag[k, z, t] = tile
     student_lse, hit = student_slopes()
     z_to_sib(zag, 6, 7)
-    got(tblk.at[pl.ds(0, R - 1)], many_recv.at[12])
+    got(tblk.at[pl.ds(0, Z - 1)], many_recv.at[12])
     t_own = town[...].reshape(PB, 128)
     top = jnp.max(t_own, axis=0, keepdims=True)
     e = jnp.exp(t_own - top)
@@ -551,7 +525,11 @@
     to_col(lambda peer: tst.at[c], tst.at[c], 13)
     pack(upt, e)
     ubuf[c] = upt[c]
-    to_col(lambda peer: upt.at[peer], ubuf.at[c], 10)
+
+    @pl.when(k == 0)
+    def _():
+        to_col(lambda peer: upt.at[peer], ubuf.at[c], 10)
+
     to_z(tag, 8)
     sq_tiles = unpack_queries()
     got(vbuf.at[pl.ds(0, C - 1)], many_recv.at[5])
@@ -566,6 +544,11 @@
     per_query = cross * inverse - (top + jnp.log(mass)) + 2.0 * student_lse - hit
     fin[r] = jnp.where(lane_group == 0, top, jnp.where(lane_group == 1, inverse, per_query))
     to_row(lambda peer: fin.at[r], fin.at[r], 11)
+
+    @pl.when(k == 1)
+    def _():
+        to_col(lambda peer: upt.at[peer], ubuf.at[c], 10)
+
     z_to_sib(tag, 8, 9)
     got(ubuf.at[pl.ds(0, C - 1)], many_recv.at[10])
     acc = jnp.zeros((8, 128), F32)
@@ -583,26 +566,22 @@
         tops = row_vector(fin, t, 0)
         inverses = row_vector(fin, t, 1)
         for b in range(GROUPS):
-            per_query = per_query + jnp.where(lane_group == 2, fin[GROUPS * t + b], 0.0)
-        slopes = zfull[t] - jnp.exp(tag[:, :, t].reshape(PB, 128) - tops) * inverses
-        slopes = jnp.concatenate(
-            [slopes[8 * (kk * Z + zz) : 8 * (kk * Z + zz) + 8] for zz in range(Z) for kk in range(2)], axis=0
-        )
+            per_query = per_query + jnp.where(lane_group == 2, fin[owner(t, b)], 0.0)
+        slopes = zfull[t] - jnp.exp(tag[t // (T // 2), :, t % (T // 2)].reshape(PB, 128) - tops) * inverses
         hi, lo = split2(slopes)
         grads = grads + nt(jnp.concatenate([sq_tiles[t]] * 2, axis=1), jnp.concatenate([hi, lo], axis=1))
     pg_ref[...] = grads * (SCALE / total)
     loss_ref[...] = jnp.zeros((1, 1), F32) + jnp.sum(per_query) / total
 
     for s in range(1, half + 1):
-        left(qbuf.at[r, mine], z_send.at[0, s - 1])
+        left(qbuf.at[z, mine], z_send.at[0, s - 1])
         if s < half:
-            left(qbuf.at[r, mine], z_send.at[1, s - 1])
+            left(qbuf.at[z, mine], z_send.at[1, s - 1])
     for j in range(len(blocks)):
         for n, part in enumerate((mine, mine, mine_a, mine_b)):
-            left(qbuf.at[r, part], xy_send.at[n, j])
-    for j in range(len(blocks) + 1):
-        left(qbuf.at[r], sib_send.at[j])
-    for n, buf, count in ((0, sqx, C), (2, sfin, R), (13, tst, C), (3, sst, C), (5, upz, C), (10, upt, C), (4, sqr, R), (11, fin, R), (12, tblk, R)):
+            left(qbuf.at[z, part], xy_send.at[n, j])
+    left(xbuf.at[k], sib_send)
+    for n, buf, count in ((0, sqx, C), (2, sfin, R), (13, tst, C), (3, sst, C), (5, upz, C), (10, upt, C), (4, sqr, R), (11, fin, R), (12, tblk, Z)):
         left(buf.at[pl.ds(0, count - 1)], many_send.at[n])
     for n, m, buf in ((1, 14, spt), (6, 7, zag), (8, 9, tag)):
         left(buf.at[0, pl.ds(0, Z - 1)], many_send.at[n])
@@ -636,12 +615,13 @@
             pltpu.SMEM((QB,), jnp.int32),
             pltpu.SMEM((8,), jnp.int32),
             pltpu.SMEM((QB,), jnp.int32),
+            pltpu.VMEM((1, 128), F32),
             pltpu.VMEM((24, QB), BF),
             pltpu.VMEM((DR, PB), BF),
             pltpu.VMEM((QB, L, 128), BF),
             pltpu.VMEM((8, LP, 128), BF),
-            pltpu.VMEM((R, QB * L, 128), BF),
-            pltpu.VMEM((LP * 8, 128), BF),
+            pltpu.VMEM((Z, QB * L, 128), BF),
+            pltpu.VMEM((2, LP * 8, 128), BF),
             pltpu.VMEM((C, 8, 128), F32),
             pltpu.VMEM((2, Z, DR, PB), BF),
             pltpu.VMEM((C, 1, 128), F32),
@@ -651,9 +631,9 @@
             pltpu.VMEM((2, Z, PB // GROUPS, 128), F32),
             pltpu.VMEM((T, PB, 128), F32),
             pltpu.VMEM((R, PR, 8, 128), F32),
-            pltpu.VMEM((R, 8, 128), F32),
-            pltpu.VMEM((2, Z, 8, 128), F32),
-            pltpu.VMEM((2, Z, T, 8, 128), F32),
+            pltpu.VMEM((Z, 2, 8, 128), F32),
+            pltpu.VMEM((Z, 2, 8, 128), F32),
+            pltpu.VMEM((2, Z, T // 2, 2, 8, 128), F32),
             pltpu.VMEM((C, 8, 128), F32),
             pltpu.VMEM((C, 8, 128), F32),
             pltpu.VMEM((C, 1, 128), F32),
@@ -666,8 +646,8 @@
             dma((2, Z // 2)),
             dma((4, hops)),
             dma((4, hops)),
-            dma((hops + 1,)),
-            dma((hops + 1,)),
+            dma,
+            dma,
             dma((15,)),
             dma((15,)),
         ],

time: 63.4 us -> 61.5 us (0.970)
  Pallas kernels: 58.8 us -> 56.9 us
    pallas_call x1, Pallas kernels: 58.8 us -> 56.9 us  [shards(): pl.pallas_call(functools.partial(kernel, R, C), out_shape=(jax.ShapeDtype...]
where the time goes in v5:
time: 61.5 us; the launch traced here: 61.3 us
  Pallas kernels  56.9 us (93%)
  between operations  2.4 us (4%)
  local copies, waits for them, and re-layouts  1.92 us (3%)
    pallas_call x1, Pallas kernels, shards(): pl.pallas_call(functools.partial(kernel, R, C), out_shape=(jax.ShapeDtype...  56.9 us
    unnamed x4, local copies, waits for them, and re-layouts  1.92 us

profile of v5, /device:TPU:1, one launch (start us, length us, event | category | flops | bytes accessed | tf_op | source)
XLA Modules:
  0.0 61.3 jit_solution(17320173565183608691)
XLA Ops:
  0.6 56.9 %distill.1 = (f32[48,128]{1,0:T(8,128)}, f32[24,32]{1,0:T(8,128)}, f32[1,1]{1,0:T(1,128)}) custom-call(bf16[32,32,128]{2,1,0:T(8,128)(2,1)} %qt_hbm.1, s32[32]{0:T(128)} %qlen_hbm.1, bf16[8,176,128]{2,1,0:T(8,128)(2,1)} %pt_hbm.1, s32[8]{0:T(128)} %plen_hbm.1, bf16[24,32]{1,0:T(8,128)(2,1)} %bitcast.8, bf16[48,128]{1,0:T(8,128)(2,1)} %bitcast.7, s32[32]{0:T(128)} %pos_hbm.1), custom_call_target="tpu_custom_call" | custom-call | tf_op jit(solution)/shard_map/distill/pallas_call | solution.py:605
  57.6 0.0 copy-start
  57.6 1.3 %copy.13 = f32[32,24]{0,1:T(8,128)} copy(f32[32,24]{0,1:T(8,128)} %bitcast.6) | data formatting | bytes 6144
  58.9 0.0 copy-done
  58.9 0.6 copy.14
Async XLA Ops:
  57.6 1.3 %copy-start = (f32[48,128]{1,0:T(8,128)S(1)}, f32[48,128]{1,0:T(8,128)}, u32[]{:S(2)}) copy-start(f32[48,128]{1,0:T(8,128)} %get-tuple-element.7) | copy-start | bytes 73732

commit v6 on v5

--- a/solution.py
+++ b/solution.py
@@ -493,16 +493,20 @@
     def _():
         pl.semaphore_wait(far_sem, R - 1 - row_place + C - 1 - col_place)
 
-    to_col(lambda peer: sqx.at[c], sqx.at[c], 0)
     to_z(spt, 1)
-    last = len(blocks) - 1
-    for j in range(len(blocks)):
-        n, w = j // 2 + 1, j % 2
-        if n < half - 1:
-            turn(n, w)
-        if j == min(3, last - 1):
+    steps = [0, *range(2, len(blocks)), 1]
+    for i, j in enumerate(steps):
+        if i == 0:
+            if half > 2:
+                turn(1, 0)
+            to_col(lambda peer: sqx.at[c], sqx.at[c], 0)
+            if half > 2:
+                turn(1, 1)
+        if i in (1, 2) and half > 3:
+            turn(2, i - 1)
+        if i == max(1, len(steps) - 4):
             z_to_sib(spt, 1, 14)
-        if j == min(4, last):
+        if i == max(1, len(steps) - 3):
             turn(half - 1, 0)
             score_student()
         xy_got(j)
@@ -586,6 +590,12 @@
     for n, m, buf in ((1, 14, spt), (6, 7, zag), (8, 9, tag)):
         left(buf.at[0, pl.ds(0, Z - 1)], many_send.at[n])
         left(buf.at[0], many_send.at[m])
+
+
+def hand_over(pg_ref, qg_ref, loss_ref, pg_out, qg_out, loss_out):
+    pg_out[...] = pg_ref[...]
+    qg_out[...] = qg_ref[...]
+    loss_out[...] = loss_ref[...]
 
 
 def shards(query_tokens, query_lengths, passage_tokens, passage_lengths, student_queries, student_passages, positives):
@@ -656,6 +666,13 @@
         ),
         name="distill",
     )(query_tokens, query_lengths, passage_tokens, passage_lengths, student_queries.T, student_passages.T, positives)
+    pg, qg, loss = pl.pallas_call(
+        hand_over,
+        out_shape=tuple(jax.ShapeDtypeStruct(a.shape, a.dtype) for a in (pg, qg, loss)),
+        in_specs=[vmem] * 3,
+        out_specs=(vmem, vmem, vmem),
+        name="hand_over",
+    )(pg, qg, loss)
     return qg.T, pg.T, loss.reshape(())
 
 

time: 61.5 us -> 59.6 us (0.969)
  local copies, waits for them, and re-layouts: 1.92 us -> 0 us
  Pallas kernels: 56.9 us -> 58.8 us
  between operations: 2.4 us -> 0.64 us
    pallas_call x0 -> x1, Pallas kernels: none -> 1.97 us  [shards(): pl.pallas_call(hand_over, out_shape=tuple((jax.ShapeDtypeStruct(a.shape,...]
    unnamed x4 -> x0, local copies, waits for them, and re-layouts: 1.92 us -> none
where the time goes in v6:
time: 59.6 us; the launch traced here: 59.4 us
  Pallas kernels  58.8 us (99%)
  between operations  0.64 us (1%)
    pallas_call x1, Pallas kernels, shards(): pl.pallas_call(functools.partial(kernel, R, C), out_shape=(jax.ShapeDtype...  56.8 us
    pallas_call x1, Pallas kernels, shards(): pl.pallas_call(hand_over, out_shape=tuple((jax.ShapeDtypeStruct(a.shape,...  1.97 us

profile of v6, /device:TPU:1, one launch (start us, length us, event | category | flops | bytes accessed | tf_op | source)
XLA Modules:
  0.0 59.4 jit_solution(3962517943377379837)
XLA Ops:
  0.6 56.8 %distill.1 = (f32[48,128]{1,0:T(8,128)}, f32[24,32]{1,0:T(8,128)}, f32[1,1]{1,0:T(1,128)}) custom-call(bf16[32,32,128]{2,1,0:T(8,128)(2,1)} %qt_hbm.1, s32[32]{0:T(128)} %qlen_hbm.1, bf16[8,176,128]{2,1,0:T(8,128)(2,1)} %pt_hbm.1, s32[8]{0:T(128)} %plen_hbm.1, bf16[24,32]{1,0:T(8,128)(2,1)} %bitcast.6, bf16[48,128]{1,0:T(8,128)(2,1)} %bitcast.5, s32[32]{0:T(128)} %pos_hbm.1), custom_call_target="tpu_custom_call" | custom-call | tf_op jit(solution)/shard_map/distill/pallas_call | solution.py:615
  57.4 2.0 %hand_over.1 = (f32[48,128]{1,0:T(8,128)}, f32[24,32]{1,0:T(8,128)}, f32[1,1]{1,0:T(1,128)}) custom-call(f32[48,128]{1,0:T(8,128)} %get-tuple-element.9.pg_ref, f32[24,32]{1,0:T(8,128)} %get-tuple-element.10.qg_ref, f32[1,1]{1,0:T(1,128)} %get-tuple-element.11.loss_ref), custom_call_target="tpu_custom_call" | custom-call | tf_op jit(solution)/shard_map/hand_over/pallas_call | solution.py:669

commit v7 on v6

--- a/solution.py
+++ b/solution.py
@@ -41,7 +41,7 @@
     qlen_hbm,
     pt_hbm,
     plen_hbm,
-    sq_hbm,
+    sq_ref,
     sp_hbm,
     pos_hbm,
     pg_ref,
@@ -51,7 +51,6 @@
     plen_ref,
     pos_ref,
     wanted_ref,
-    sq_ref,
     sp_ref,
     qraw,
     praw,
@@ -181,7 +180,6 @@
                 (qlen_hbm, qlen_ref),
                 (pt_hbm, praw),
                 (plen_hbm, plen_ref),
-                (sq_hbm, sq_ref),
                 (sp_hbm, sp_ref),
                 (pos_hbm, pos_ref),
             )
@@ -205,7 +203,6 @@
 
 
     inputs[4].wait()
-    inputs[5].wait()
     qa = lax.broadcasted_iota(jnp.int32, (QB, 128), 0)
     qb = lax.broadcasted_iota(jnp.int32, (QB, 128), 1)
     sq_wide = nn(sq_ref[...], (qa == lax.rem(qb, QB)).astype(BF))
@@ -218,7 +215,7 @@
         [sp_wide[24 * u + 8 * g : 24 * u + 8 * g + 8] for g in range(3) for u in range(PR)], axis=0
     ).astype(BF)
 
-    inputs[6].wait()
+    inputs[5].wait()
     wanted = jnp.zeros((1, 128), F32)
     within = lax.rem(lane, QB)
     for i in range(QB):
@@ -619,14 +616,13 @@
             jax.ShapeDtypeStruct((24, QB), F32),
             jax.ShapeDtypeStruct((1, 1), F32),
         ),
-        in_specs=[hbm] * 7,
+        in_specs=[hbm] * 4 + [vmem] + [hbm] * 2,
         out_specs=(vmem, vmem, vmem),
         scratch_shapes=[
             pltpu.SMEM((QB,), jnp.int32),
             pltpu.SMEM((8,), jnp.int32),
             pltpu.SMEM((QB,), jnp.int32),
             pltpu.VMEM((1, 128), F32),
-            pltpu.VMEM((24, QB), BF),
             pltpu.VMEM((DR, PB), BF),
             pltpu.VMEM((QB, L, 128), BF),
             pltpu.VMEM((8, LP, 128), BF),

time: 59.6 us -> 60.3 us (1.012)
  Pallas kernels: 58.8 us -> 59.5 us
    pallas_call x1, Pallas kernels: 56.8 us -> 57.5 us  [shards(): pl.pallas_call(functools.partial(kernel, R, C), out_shape=(jax.ShapeDtype...]
where the time goes in v7:
time: 60.3 us; the launch traced here: 60.1 us
  Pallas kernels  59.5 us (99%)
  between operations  0.64 us (1%)
    pallas_call x1, Pallas kernels, shards(): pl.pallas_call(functools.partial(kernel, R, C), out_shape=(jax.ShapeDtype...  57.5 us
    pallas_call x1, Pallas kernels, shards(): pl.pallas_call(hand_over, out_shape=tuple((jax.ShapeDtypeStruct(a.shape,...  1.97 us

profile of v7, /device:TPU:1, one launch (start us, length us, event | category | flops | bytes accessed | tf_op | source)
XLA Modules:
  0.0 60.1 jit_solution(17334334024362734197)
XLA Ops:
  0.6 57.5 %distill.1 = (f32[48,128]{1,0:T(8,128)}, f32[24,32]{1,0:T(8,128)}, f32[1,1]{1,0:T(1,128)}) custom-call(bf16[32,32,128]{2,1,0:T(8,128)(2,1)} %qt_hbm.1, s32[32]{0:T(128)} %qlen_hbm.1, bf16[8,176,128]{2,1,0:T(8,128)(2,1)} %pt_hbm.1, s32[8]{0:T(128)} %plen_hbm.1, bf16[24,32]{1,0:T(8,128)(2,1)} %bitcast.6, bf16[48,128]{1,0:T(8,128)(2,1)} %bitcast.5, s32[32]{0:T(128)} %pos_hbm.1), custom_call_target="tpu_custom_call" | custom-call | tf_op jit(solution)/shard_map/distill/pallas_call | solution.py:612
  58.1 2.0 %hand_over.1 = (f32[48,128]{1,0:T(8,128)}, f32[24,32]{1,0:T(8,128)}, f32[1,1]{1,0:T(1,128)}) custom-call(f32[48,128]{1,0:T(8,128)} %get-tuple-element.9.pg_ref, f32[24,32]{1,0:T(8,128)} %get-tuple-element.10.qg_ref, f32[1,1]{1,0:T(1,128)} %get-tuple-element.11.loss_ref), custom_call_target="tpu_custom_call" | custom-call | tf_op jit(solution)/shard_map/hand_over/pallas_call | solution.py:665
